TPU v7x, 32 devices: a whole 2x2x4 slice. The times are simulated.
32 devices in a mesh: dp: 4 (over y, x), expert: 8 (over z, core).
Axes of the slice: x: 2, y: 2, z: 4, core: 2. Of those that a mesh axis runs over, the one named last changes fastest.
Arguments:
- tokens: bfloat16 [4096, 1024], P(('dp', 'expert')), may hold values from -6 to 6
- cotangent: bfloat16 [4096, 1024], P(('dp', 'expert')), may hold values from -6 to 6
- expert_ids: int32 [4096, 8], P(('dp', 'expert')), may hold values from 0 to 15, all different within a row; in each aligned block of 128 rows (0 to 127, 128 to 255, ...) at most 80 rows name the same one
- gate_probs: bfloat16 [4096, 8], P(('dp', 'expert')), may hold values from 0.049804688 to 0.5
- gate_up: bfloat16 [16, 1024, 1024], P('expert', 'dp'), may hold values from -0.1875 to 0.1875
- down_proj: bfloat16 [16, 512, 1024], P('expert', 'dp'), may hold values from -0.25 to 0.25
Outputs:
- grad_tokens: bfloat16 [4096, 1024], P(('dp', 'expert'))
- grad_gates: bfloat16 [4096, 8], P(('dp', 'expert'))
- grad_gate_up: float32 [16, 1024, 1024], P('expert', 'dp')
- grad_down: float32 [16, 512, 1024], P('expert', 'dp')
Inputs may be any that keep to these rules, and one draw needn't show every extreme that they name: `expert_ids`: each token names 8 different experts. Among the 128 tokens of one device (aligned blocks of rows) no expert is named more than 80 times, and in every draw some expert is named exactly 80 times by the tokens of some device.
All inputs are finite; a program needn't handle non-finite values.
Results may differ from a plain program's by a relative error of at most 0.0058.
Values may be sent and summed in bfloat16 or wider, within the bound.
A program may use at most 128 MiB of HBM per device.

v0:
```python
import jax
import jax.numpy as jnp
from jax import lax
from jax.sharding import PartitionSpec as P

TOP = 8
EXP_DEV = 2


def slot_index(expert_ids, experts_all, capacity):
    flat_ids = expert_ids.reshape(-1)
    onehot = (flat_ids[:, None] == jnp.arange(experts_all, dtype=jnp.int32)[None, :]).astype(
        jnp.int32
    )
    before = jnp.cumsum(onehot, axis=0) - onehot
    slot_rank = jnp.sum(before * onehot, axis=1)
    return flat_ids * capacity + slot_rank


def expert_grads(routed_x, routed_dy, routed_gate, w_in, w_out):
    pre_act = jnp.einsum("jrd,jdf->jrf", routed_x, w_in, preferred_element_type=jnp.float32)
    hidden = w_out.shape[1]
    gate_pre = pre_act[..., :hidden]
    up_pre = pre_act[..., hidden:]
    sigmoid_h = jax.nn.sigmoid(gate_pre)
    silu_h = gate_pre * sigmoid_h
    activation = silu_h * up_pre
    raw_grad = jnp.einsum("jrd,jfd->jrf", routed_dy, w_out, preferred_element_type=jnp.float32)
    gate_col = routed_gate.astype(jnp.float32)[..., None]
    act_grad = gate_col * raw_grad
    grad_gate = act_grad * up_pre * sigmoid_h * (1.0 + gate_pre * (1.0 - sigmoid_h))
    grad_up = act_grad * silu_h
    pre_grad = jnp.concatenate([grad_gate, grad_up], axis=-1).astype(jnp.bfloat16)
    scaled_act = (gate_col * activation).astype(jnp.bfloat16)
    slot_dx = jnp.einsum("jrf,jdf->jrd", pre_grad, w_in, preferred_element_type=jnp.float32).astype(
        jnp.bfloat16
    )
    slot_gate = jnp.sum(activation * raw_grad, axis=-1).astype(jnp.bfloat16)
    return (pre_grad, scaled_act, slot_dx, slot_gate)


def row_terms(left_side, right_side, row_count):
    summed = jnp.einsum("jrc,jrf->cjf", left_side, right_side, preferred_element_type=jnp.float32)
    return summed.reshape(row_count, -1)


def body(tokens, cotangent, expert_ids, gate_probs, gate_up, down_proj):
    tok_count, width = tokens.shape
    owners = lax.axis_size("expert")
    experts_all = EXP_DEV * owners
    capacity = 5 * tok_count * TOP // (4 * experts_all)
    slot_dest = slot_index(expert_ids, experts_all, capacity)
    buffer_rows = experts_all * capacity
    send_x = (
        jnp.zeros((buffer_rows, width), jnp.bfloat16)
        .at[slot_dest]
        .set(jnp.repeat(tokens, TOP, axis=0))
    )
    send_dy = (
        jnp.zeros((buffer_rows, width), jnp.bfloat16)
        .at[slot_dest]
        .set(jnp.repeat(cotangent, TOP, axis=0))
    )
    send_gate = jnp.zeros((buffer_rows,), jnp.bfloat16).at[slot_dest].set(gate_probs.reshape(-1))
    block_shape = (owners, EXP_DEV, capacity, width)
    recv_x, recv_dy, recv_gate = (
        lax.all_to_all(
            send_x.reshape(block_shape), "expert", split_axis=0, concat_axis=2, tiled=True
        ),
        lax.all_to_all(
            send_dy.reshape(block_shape), "expert", split_axis=0, concat_axis=2, tiled=True
        ),
        lax.all_to_all(
            send_gate.reshape(owners, EXP_DEV, capacity),
            "expert",
            split_axis=0,
            concat_axis=2,
            tiled=True,
        ),
    )
    routed_x = recv_x[0]
    routed_dy = recv_dy[0]
    routed_gate = recv_gate[0]
    rows_in = gate_up.shape[1]
    rows_out = down_proj.shape[1]
    w_in, w_out = (
        lax.all_gather(gate_up, "dp", axis=1, tiled=True),
        lax.all_gather(down_proj, "dp", axis=1, tiled=True),
    )
    pre_grad, scaled_act, slot_dx, slot_gate = expert_grads(
        routed_x, routed_dy, routed_gate, w_in, w_out
    )
    summed_in = lax.psum_scatter(
        row_terms(routed_x, pre_grad, rows_in * lax.axis_size("dp")),
        "dp",
        scatter_dimension=0,
        tiled=True,
    )
    summed_out = lax.psum_scatter(
        row_terms(scaled_act, routed_dy, rows_out * lax.axis_size("dp")),
        "dp",
        scatter_dimension=0,
        tiled=True,
    )
    grad_gate_up = summed_in.reshape(rows_in, EXP_DEV, -1).transpose(1, 0, 2)
    grad_down = summed_out.reshape(rows_out, EXP_DEV, -1).transpose(1, 0, 2)
    back_dx, back_gate = (
        lax.all_to_all(slot_dx[None], "expert", split_axis=2, concat_axis=0, tiled=True),
        lax.all_to_all(slot_gate[None], "expert", split_axis=2, concat_axis=0, tiled=True),
    )
    slot_rows = back_dx.reshape(buffer_rows, width)[slot_dest]
    grad_tokens = jnp.sum(
        slot_rows.reshape(tok_count, TOP, width).astype(jnp.float32), axis=1
    ).astype(jnp.bfloat16)
    grad_gates = back_gate.reshape(buffer_rows)[slot_dest].reshape(tok_count, TOP)
    return (grad_tokens, grad_gates, grad_gate_up, grad_down)


def solution(mesh):
    placed = (
        P(("dp", "expert"), None),
        P(("dp", "expert"), None),
        P(("dp", "expert"), None),
        P(("dp", "expert"), None),
        P("expert", "dp", None),
        P("expert", "dp", None),
    )
    return jax.shard_map(
        body,
        mesh=mesh,
        in_specs=placed,
        out_specs=(
            P(("dp", "expert"), None),
            P(("dp", "expert"), None),
            P("expert", "dp", None),
            P("expert", "dp", None),
        ),
        check_vma=False,
    )
```

profile of v0, /device:TPU:0, one launch (start us, length us, event | category | flops | bytes accessed | tf_op | source)
XLA Modules:
  0.0 331.5 jit_solution(2092867298496987495)
XLA Ops:
  7.9 0.8 copy.76
  8.9 0.8 copy.80
  10.0 4.5 %reduce-window.6 = s32[16,8,128]{2,1,0:T(8,128)S(1)} reduce-window(s32[16,8,128]{2,1,0:T(8,128)S(1)} %fusion.15, s32[]{:T(128)} %constant.8.clone.1), window={size=1x1x128 pad=0_0x0_0x127_0}, to_apply=%region_0.0 | reduce-window | flops 2080768 | bytes 131076 | tf_op jit(solution)/shard_map/reduce-window
  15.0 7.6 %scatter_custom_fusion = bf16[1280]{0:T(1024)(128)(2,1)S(1)} fusion(s32[1024]{0:T(1024)S(1)} %bitcast.95, bf16[1024]{0:T(1024)(128)(2,1)S(1)} %reshape.155, bf16[]{:T(256)} %constant.6.clone.1), kind=kCustom, calls=%fused_computation.39 | custom fusion | bytes 2562 | tf_op jit(solution)/shard_map/scatter | solution.py:64
  23.3 6.3 %all-to-all-start = ((bf16[8,2,80]{2,1,0:T(2,128)(2,1)}), bf16[8,2,80]{2,1,0:T(2,128)(2,1)S(1)}, u32[]{:S(2)}, u32[]{:S(2)}) async-start(bf16[8,2,80]{2,1,0:T(2,128)(2,1)} %reshape.120), calls=%async_computation | async-start | bytes 8192 | tf_op jit(solution)/shard_map/all_to_all | solution.py:73
  29.6 7.1 %scatter_custom_fusion.2 = bf16[1280,1024]{1,0:T(8,128)(2,1)} fusion(s32[1024]{0:T(1024)S(1)} %bitcast.96, bf16[]{:T(256)} %constant.6.clone.1, bf16[128,1024]{1,0:T(8,128)(2,1)S(1)} %copy-done), kind=kCustom, calls=%fused_computation.15 | custom fusion | bytes 2883586 | tf_op jit(solution)/shard_map/scatter | solution.py:57
  36.7 5.2 %all-to-all-start.2 = ((bf16[8,2,80,1024]{3,2,1,0:T(8,128)(2,1)}), bf16[8,2,80,1024]{3,2,1,0:T(8,128)(2,1)S(1)}, u32[]{:S(2)}, u32[]{:S(2)}) async-start(bf16[8,2,80,1024]{3,2,1,0:T(8,128)(2,1)} %bitcast.83), calls=%async_computation.2 | async-start | bytes 5242880 | tf_op jit(solution)/shard_map/all_to_all | solution.py:67
  42.7 7.1 %scatter_custom_fusion.1 = bf16[1280,1024]{1,0:T(8,128)(2,1)} fusion(s32[1024]{0:T(1024)S(1)} %bitcast.97, bf16[]{:T(256)} %constant.6.clone.1, bf16[128,1024]{1,0:T(8,128)(2,1)S(1)} %copy-done.4), kind=kCustom, calls=%fused_computation.17 | custom fusion | bytes 2883586 | tf_op jit(solution)/shard_map/scatter | solution.py:62
  49.8 52.4 %all-to-all-done.2 = bf16[8,2,80,1024]{3,2,1,0:T(8,128)(2,1)S(1)} async-done(((bf16[8,2,80,1024]{3,2,1,0:T(8,128)(2,1)}), bf16[8,2,80,1024]{3,2,1,0:T(8,128)(2,1)S(1)}, u32[]{:S(2)}, u32[]{:S(2)}) %all-to-all-start.2) | async-done | bytes 2621472 | tf_op jit(solution)/shard_map/all_to_all | solution.py:67
  102.3 4.4 %all-to-all-start.1 = ((bf16[8,2,80,1024]{3,2,1,0:T(8,128)(2,1)}), bf16[8,2,80,1024]{3,2,1,0:T(8,128)(2,1)}, u32[]{:S(2)}, u32[]{:S(2)}) async-start(bf16[8,2,80,1024]{3,2,1,0:T(8,128)(2,1)} %bitcast.81), calls=%async_computation.1 | async-start | bytes 5242880 | tf_op jit(solution)/shard_map/all_to_all | solution.py:70
  107.6 1.9 copy.83
  109.5 57.5 %all-to-all-done.1 = bf16[8,2,80,1024]{3,2,1,0:T(8,128)(2,1)} async-done(((bf16[8,2,80,1024]{3,2,1,0:T(8,128)(2,1)}), bf16[8,2,80,1024]{3,2,1,0:T(8,128)(2,1)}, u32[]{:S(2)}, u32[]{:S(2)}) %all-to-all-start.1) | async-done | bytes 2621472 | tf_op jit(solution)/shard_map/all_to_all | solution.py:70
  167.0 3.7 %copy.82 = bf16[1,2,8,80,1024]{4,3,2,1,0:T(8,128)(2,1)} copy(bf16[1,2,8,80,1024]{4,3,1,2,0:T(8,128)(2,1)} %bitcast.9) | data formatting | bytes 5242880 | tf_op jit(solution)/shard_map/all_to_all | solution.py:70
  170.7 5.6 %fusion.21 = f32[2,640,1024]{1,2,0:T(8,128)S(1)} fusion(bf16[2,640,1024]{2,1,0:T(8,128)(2,1)S(1)} %bitcast.86, bf16[2,1024,1024]{2,1,0:T(8,128)(2,1)} %all-gather.5.cloned.1.call-done), kind=kOutput, calls=%fused_computation.43 | convolution fusion | flops 2684354560 | bytes 12058624 | tf_op jit(solution)/shard_map/jrd,jdf->jrf/dot_general | solution.py:21
  176.3 4.4 %fusion.6 = f32[2,1024,512]{2,1,0:T(8,128)} fusion(bf16[2,640,1024]{2,1,0:T(8,128)(2,1)S(1)} %bitcast.89, f32[2,640]{1,0:T(2,128)S(1)} %reshape.133, f32[2,640,1024]{1,2,0:T(8,128)S(1)} %fusion.21), kind=kOutput, calls=%fused_computation.20 | convolution fusion | flops 1346764800 | bytes 12063744 | tf_op jit(solution)/shard_map/jrc,jrf->cjf/dot_general | solution.py:43
  180.8 6.7 %multiply_convert_fusion.2 = (bf16[2,640,512]{1,2,0:T(8,128)(2,1)S(1)}, bf16[2,640,512]{1,2,0:T(8,128)(2,1)S(1)}, bf16[2,640]{1,0:T(2,128)(2,1)S(1)}) fusion(f32[2,640,1024]{1,2,0:T(8,128)} %copy-done.9, f32[2,640]{1,0:T(2,128)S(1)} %reshape.133, bf16[2,640,1024]{2,1,0:T(8,128)(2,1)} %bitcast.88, bf16[2,512,1024]{2,1,0:T(8,128)(2,1)} %all-gather.3.cloned.1.call-done), kind=kOutput, calls=%fused_computation.10 | convolution fusion | flops 1353317120 | bytes 12590592 | tf_op jit(solution)/shard_map/jrd,jfd->jrf/dot_general | solution.py:28
  187.5 5.6 %fusion.5 = f32[2,1024,1024]{2,1,0:T(8,128)} fusion(bf16[2,640,1024]{2,1,0:T(8,128)(2,1)S(1)} %bitcast.87, bf16[2,640,512]{1,2,0:T(8,128)(2,1)S(1)} %get-tuple-element.21, bf16[2,640,512]{1,2,0:T(8,128)(2,1)S(1)} %get-tuple-element.20), kind=kOutput, calls=%fused_computation.19 | convolution fusion | flops 2689597440 | bytes 13631488 | tf_op jit(solution)/shard_map/jrc,jrf->cjf/dot_general | solution.py:43
  193.2 1.0 copy.89
  194.2 3.7 %all-to-all-start.4 = ((bf16[1,2,640]{1,0,2:T(2,128)(2,1)}), bf16[1,2,640]{1,0,2:T(2,128)(2,1)S(1)}, u32[]{:S(2)}, u32[]{:S(2)}) async-start(bf16[1,2,640]{1,0,2:T(2,128)(2,1)} %copy.89), calls=%async_computation.4 | async-start | bytes 655360 | tf_op jit(solution)/shard_map/all_to_all | solution.py:109
  197.8 5.7 %convert_bitcast_fusion = bf16[1,2,640,1024]{3,2,1,0:T(8,128)(2,1)S(1)} fusion(bf16[2,1024,1024]{2,1,0:T(8,128)(2,1)} %all-gather.5.cloned.1.call-done, bf16[2,640,512]{1,2,0:T(8,128)(2,1)S(1)} %copy-done.8, bf16[2,640,512]{1,2,0:T(8,128)(2,1)S(1)} %copy-done.6), kind=kOutput, calls=%fused_computation.8 | convolution fusion | flops 2690908160 | bytes 9437184 | tf_op jit(solution)/shard_map/jrf,jdf->jrd/dot_general | solution.py:35
  203.5 4.3 %copy.87 = bf16[1,2,640,1024]{3,1,0,2:T(2,128)(2,1)} copy(bf16[1,2,640,1024]{3,2,1,0:T(8,128)(2,1)S(1)} %convert_bitcast_fusion) | data formatting | bytes 5242880 | tf_op jit(solution)/shard_map/broadcast_in_dim | solution.py:108
  207.8 0.9 all-to-all-done.4
  208.7 3.9 %all-to-all-start.3 = ((bf16[1,2,640,1024]{3,1,0,2:T(2,128)(2,1)}), bf16[1,2,640,1024]{3,1,0,2:T(2,128)(2,1)S(1)}, u32[]{:S(2)}, u32[]{:S(2)}) async-start(bf16[1,2,640,1024]{3,1,0,2:T(2,128)(2,1)} %copy.87), calls=%async_computation.3 | async-start | bytes 5242880 | tf_op jit(solution)/shard_map/all_to_all | solution.py:108
  212.9 6.8 %gather_fusion.1 = bf16[1024]{0:T(1024)(128)(2,1)S(1)} fusion(bf16[1280]{0:T(1024)(128)(2,1)S(1)} %reshape.127, s32[1024]{0:T(1024)S(1)} %broadcast_clamp_fusion), kind=kCustom, calls=%fused_computation.1 | custom fusion | bytes 8192 | tf_op jit(solution)/shard_map/gather | solution.py:115
  220.4 52.4 %all-to-all-done.3 = bf16[1,2,640,1024]{3,1,0,2:T(2,128)(2,1)S(1)} async-done(((bf16[1,2,640,1024]{3,1,0,2:T(2,128)(2,1)}), bf16[1,2,640,1024]{3,1,0,2:T(2,128)(2,1)S(1)}, u32[]{:S(2)}, u32[]{:S(2)}) %all-to-all-start.3) | async-done | bytes 2621472 | tf_op jit(solution)/shard_map/all_to_all | solution.py:108
  272.8 1.6 copy-done.1
  274.4 2.5 copy.88
  277.0 5.3 %gather_fusion = bf16[1024,1024]{1,0:T(8,128)(2,1)} fusion(bf16[1280,1024]{1,0:T(8,128)(2,1)S(1)} %bitcast.79, s32[1024]{0:T(1024)S(1)} %broadcast_clamp_fusion), kind=kCustom, calls=%fused_computation | custom fusion | bytes 4198400 | tf_op jit(solution)/shard_map/gather | solution.py:111
  282.3 3.7 %bitcast_reduce_fusion = bf16[128,1024]{1,0:T(8,128)(2,1)} fusion(bf16[1024,1024]{1,0:T(8,128)(2,1)} %gather_fusion), kind=kLoop, calls=%fused_computation.14 | loop fusion | flops 917504 | bytes 2359296 | tf_op jit(solution)/shard_map/reduce_sum | solution.py:112
  286.0 2.5 copy.96
  288.6 33.5 %reduce-scatter.3.cloned.1.call-done = f32[256,2048]{0,1:T(8,128)} async-done(((f32[1024,2048]{0,1:T(8,128)}), f32[256,2048]{0,1:T(8,128)}) %reduce-scatter.3.cloned.1.call-update) | async-done | bytes 2097168 | tf_op jit(solution)/shard_map/reduce_scatter | solution.py:93
  322.0 2.9 copy.95
  (57 shorter events, 5.1 us)
Async XLA Ops:
  7.2 22.4 %copy-start = (bf16[128,1024]{1,0:T(8,128)(2,1)S(1)}, bf16[128,1024]{1,0:T(8,128)(2,1)}, u32[]{:S(2)}) copy-start(bf16[128,1024]{1,0:T(8,128)(2,1)} %param.6) | copy-start | bytes 786436
  23.3 13.5 %all-to-all-start = ((bf16[8,2,80]{2,1,0:T(2,128)(2,1)}), bf16[8,2,80]{2,1,0:T(2,128)(2,1)S(1)}, u32[]{:S(2)}, u32[]{:S(2)}) async-start(bf16[8,2,80]{2,1,0:T(2,128)(2,1)} %reshape.120), calls=%async_computation | async-start | bytes 8192 | tf_op jit(solution)/shard_map/all_to_all | solution.py:73
  36.7 6.0 %copy-start.4 = (bf16[128,1024]{1,0:T(8,128)(2,1)S(1)}, bf16[128,1024]{1,0:T(8,128)(2,1)}, u32[]{:S(2)}) copy-start(bf16[128,1024]{1,0:T(8,128)(2,1)} %param.7) | copy-start | bytes 786436
  36.7 65.5 %all-to-all-start.2 = ((bf16[8,2,80,1024]{3,2,1,0:T(8,128)(2,1)}), bf16[8,2,80,1024]{3,2,1,0:T(8,128)(2,1)S(1)}, u32[]{:S(2)}, u32[]{:S(2)}) async-start(bf16[8,2,80,1024]{3,2,1,0:T(8,128)(2,1)} %bitcast.83), calls=%async_computation.2 | async-start | bytes 5242880 | tf_op jit(solution)/shard_map/all_to_all | solution.py:67
  42.0 128.7 %all-gather.5.cloned.1.call-start = ((), (), s32[]{:S(2)}) async-start(), calls=%async_computation.8 | async-start | bytes 5242880 | tf_op jit(solution)/shard_map/all_gather | solution.py:87
  102.3 64.7 %all-to-all-start.1 = ((bf16[8,2,80,1024]{3,2,1,0:T(8,128)(2,1)}), bf16[8,2,80,1024]{3,2,1,0:T(8,128)(2,1)}, u32[]{:S(2)}, u32[]{:S(2)}) async-start(bf16[8,2,80,1024]{3,2,1,0:T(8,128)(2,1)} %bitcast.81), calls=%async_computation.1 | async-start | bytes 5242880 | tf_op jit(solution)/shard_map/all_to_all | solution.py:70
  106.7 74.1 %all-gather.3.cloned.1.call-start = ((), (), s32[]{:S(2)}) async-start(), calls=%async_computation.7 | async-start | bytes 2621440 | tf_op jit(solution)/shard_map/all_gather | solution.py:88
  107.4 178.6 %reduce-scatter.5.cloned.1.call-start = ((), (), s32[]{:S(2)}) async-start(), calls=%async_computation.10 | async-start | bytes 5242880 | tf_op jit(solution)/shard_map/reduce_scatter | solution.py:99
  167.0 3.7 %copy-start.2 = (bf16[1,2,8,80,1024]{4,3,2,1,0:T(8,128)(2,1)S(1)}, bf16[1,2,8,80,1024]{4,3,2,1,0:T(8,128)(2,1)}, u32[]{:S(2)}) copy-start(bf16[1,2,8,80,1024]{4,3,2,1,0:T(8,128)(2,1)} %copy.83) | copy-start | bytes 7864324
  170.7 5.6 %copy-start.3 = (bf16[1,2,8,80,1024]{4,3,2,1,0:T(8,128)(2,1)S(1)}, bf16[1,2,8,80,1024]{4,3,2,1,0:T(8,128)(2,1)}, u32[]{:S(2)}) copy-start(bf16[1,2,8,80,1024]{4,3,2,1,0:T(8,128)(2,1)} %copy.82) | copy-start | bytes 7864324
  176.3 4.4 %copy-start.9 = (f32[2,640,1024]{1,2,0:T(8,128)}, f32[2,640,1024]{1,2,0:T(8,128)S(1)}, u32[]{:S(2)}) copy-start(f32[2,640,1024]{1,2,0:T(8,128)S(1)} %fusion.21) | copy-start | bytes 15728644
  180.7 141.3 %reduce-scatter.3.cloned.1.call-start = ((), (), s32[]{:S(2)}) async-start(), calls=%async_computation.9 | async-start | bytes 10485760 | tf_op jit(solution)/shard_map/reduce_scatter | solution.py:93
  187.5 5.6 %copy-start.5 = (bf16[2,640,512]{1,2,0:T(8,128)(2,1)}, bf16[2,640,512]{1,2,0:T(8,128)(2,1)S(1)}, u32[]{:S(2)}) copy-start(bf16[2,640,512]{1,2,0:T(8,128)(2,1)S(1)} %get-tuple-element.20) | copy-start | bytes 3932164
  187.5 5.6 %copy-start.7 = (bf16[2,640,512]{1,2,0:T(8,128)(2,1)}, bf16[2,640,512]{1,2,0:T(8,128)(2,1)S(1)}, u32[]{:S(2)}) copy-start(bf16[2,640,512]{1,2,0:T(8,128)(2,1)S(1)} %get-tuple-element.21) | copy-start | bytes 3932164
  193.2 4.7 %copy-start.6 = (bf16[2,640,512]{1,2,0:T(8,128)(2,1)S(1)}, bf16[2,640,512]{1,2,0:T(8,128)(2,1)}, u32[]{:S(2)}) copy-start(bf16[2,640,512]{1,2,0:T(8,128)(2,1)} %copy-done.5) | copy-start | bytes 3932164
  193.2 4.7 %copy-start.8 = (bf16[2,640,512]{1,2,0:T(8,128)(2,1)S(1)}, bf16[2,640,512]{1,2,0:T(8,128)(2,1)}, u32[]{:S(2)}) copy-start(bf16[2,640,512]{1,2,0:T(8,128)(2,1)} %copy-done.7) | copy-start | bytes 3932164
  194.2 14.5 %all-to-all-start.4 = ((bf16[1,2,640]{1,0,2:T(2,128)(2,1)}), bf16[1,2,640]{1,0,2:T(2,128)(2,1)S(1)}, u32[]{:S(2)}, u32[]{:S(2)}) async-start(bf16[1,2,640]{1,0,2:T(2,128)(2,1)} %copy.89), calls=%async_computation.4 | async-start | bytes 655360 | tf_op jit(solution)/shard_map/all_to_all | solution.py:109
  208.7 64.2 %all-to-all-start.3 = ((bf16[1,2,640,1024]{3,1,0,2:T(2,128)(2,1)}), bf16[1,2,640,1024]{3,1,0,2:T(2,128)(2,1)S(1)}, u32[]{:S(2)}, u32[]{:S(2)}) async-start(bf16[1,2,640,1024]{3,1,0,2:T(2,128)(2,1)} %copy.87), calls=%async_computation.3 | async-start | bytes 5242880 | tf_op jit(solution)/shard_map/all_to_all | solution.py:108
  272.8 1.6 copy-start.1
Sparse Core Ops, SparseCore 0:
  44.6 54.1 all-gather.4
  109.4 36.6 all-gather.2
  180.8 51.5 reduce-scatter.4
  235.7 86.3 reduce-scatter.2
where the time goes:
time: 332 us; the launch traced here: 331 us
  waiting for transfers between devices  198 us (60%)
  local copies, waits for them, and re-layouts  58.6 us (18%)
  matrix products  27.9 us (8%)
  starting transfers between devices  23.6 us (7%)
  between operations  14 us (4%)
  other arithmetic  9.15 us (3%)
    all_to_all x1, waiting for transfers between devices, body(): lax.all_to_all(send_dy.reshape(block_shape), 'expert', split_axis=0, conc...  57.5 us
    all_to_all x1, waiting for transfers between devices, body(): lax.all_to_all(send_x.reshape(block_shape), 'expert', split_axis=0, conca...  52.4 us
    all_to_all x1, waiting for transfers between devices, body(): lax.all_to_all(slot_dx[None], 'expert', split_axis=2, concat_axis=0, tile...  52.4 us
    reduce_scatter x1, waiting for transfers between devices, body(): lax.psum_scatter(row_terms(routed_x, pre_grad, rows_in * lax.axis_size('d...  33.5 us
    dot_general x2, matrix products, row_terms(): jnp.einsum('jrc,jrf->cjf', left_side, right_side, preferred_element_type=...  10 us
    unnamed x25, local copies, waits for them, and re-layouts  9.27 us
    scatter x1, local copies, waits for them, and re-layouts, body(): jnp.zeros((buffer_rows,), jnp.bfloat16).at[slot_dest]  7.59 us
    scatter x1, local copies, waits for them, and re-layouts, body(): send_x = jnp.zeros((buffer_rows, width), jnp.bfloat16).at[slot_dest].set(...  7.13 us
  transfers between devices with their start and end apart: 9, of which 5 were waited for; matrix products, arithmetic and copies ran while one was open for 23% of the time, Pallas kernels for 0%

commit v1 on v0

v1 whole, which is shorter than its diff:
```python
import jax
import jax.numpy as jnp
from jax import lax
from jax.sharding import PartitionSpec as P

EXP_DEV = 2


def body(tokens, cotangent, expert_ids, gate_probs, gate_up, down_proj):
    owners = lax.axis_size("expert")
    experts_all = EXP_DEV * owners
    dp = lax.axis_size("dp")
    rows_in, rows_out = gate_up.shape[1], down_proj.shape[1]
    width, hidden = tokens.shape[1], rows_out * dp
    tok_count = tokens.shape[0]
    chosen = expert_ids[:, :, None] == jnp.arange(experts_all, dtype=jnp.int32)
    dense = jnp.sum(jnp.where(chosen, gate_probs[:, :, None].astype(jnp.float32), 0.0), axis=1)
    dense = dense.astype(jnp.bfloat16)
    all_x = lax.all_gather(tokens, "expert", axis=0, tiled=True)
    all_dy = lax.all_gather(cotangent, "expert", axis=0, tiled=True)
    gates = lax.all_to_all(dense, "expert", split_axis=1, concat_axis=0, tiled=True)
    w_in = lax.all_gather(gate_up, "dp", axis=1, tiled=True)
    w_out = lax.all_gather(down_proj, "dp", axis=1, tiled=True)
    pres, acts, gate_sums = [], [], []
    for j in range(EXP_DEV):
        pre_act = jnp.dot(all_x, w_in[j], preferred_element_type=jnp.float32)
        gate_pre, up_pre = pre_act[:, :hidden], pre_act[:, hidden:]
        sig = jax.nn.sigmoid(gate_pre)
        silu = gate_pre * sig
        act = silu * up_pre
        raw = lax.dot_general(
            all_dy, w_out[j], (((1,), (1,)), ((), ())), preferred_element_type=jnp.float32
        )
        g = gates[:, j : j + 1].astype(jnp.float32)
        act_grad = g * raw
        grad_gate = act_grad * up_pre * sig * (1.0 + gate_pre * (1.0 - sig))
        grad_up = act_grad * silu
        pres.append(jnp.concatenate([grad_gate, grad_up], axis=-1).astype(jnp.bfloat16))
        acts.append((g * act).astype(jnp.bfloat16))
        gate_sums.append(jnp.sum(act * raw, axis=-1, keepdims=True).astype(jnp.bfloat16))

    def scatter(left, right):
        full = lax.dot_general(
            left, right, (((0,), (0,)), ((), ())), preferred_element_type=jnp.float32
        ).astype(jnp.bfloat16)
        return lax.psum_scatter(full, "dp", scatter_dimension=0, tiled=True).astype(jnp.float32)

    grad_gate_up = jnp.stack([scatter(all_x, pres[j]) for j in range(EXP_DEV)])
    grad_down = jnp.stack([scatter(acts[j], all_dy) for j in range(EXP_DEV)])
    dx = sum(
        lax.dot_general(
            pres[j], w_in[j], (((1,), (1,)), ((), ())), preferred_element_type=jnp.float32
        )
        for j in range(EXP_DEV)
    ).astype(jnp.bfloat16)
    grad_tokens = lax.psum_scatter(dx, "expert", scatter_dimension=0, tiled=True)
    back = lax.all_to_all(
        jnp.concatenate(gate_sums, axis=1), "expert", split_axis=0, concat_axis=1, tiled=True
    )
    grad_gates = jnp.sum(
        jnp.where(chosen, back[:, None, :].astype(jnp.float32), 0.0), axis=2
    ).astype(jnp.bfloat16)
    return (grad_tokens, grad_gates, grad_gate_up, grad_down)


def solution(mesh):
    tok = P(("dp", "expert"), None)
    wgt = P("expert", "dp", None)
    return jax.shard_map(
        body,
        mesh=mesh,
        in_specs=(tok, tok, tok, tok, wgt, wgt),
        out_specs=(tok, tok, wgt, wgt),
        check_vma=False,
    )
```

time: 332 us -> 374 us (1.13)
  waiting for transfers between devices: 198 us -> 285 us
  local copies, waits for them, and re-layouts: 58.6 us -> 6.68 us
  starting transfers between devices: 23.6 us -> 3.85 us
  matrix products: 27.9 us -> 44.4 us
  blocking collectives: 0 us -> 7.91 us
    all_to_all x5 -> x1, waiting for transfers between devices: 163 us -> 5.34 us  [body(): lax.all_to_all(jnp.concatenate(gate_sums, axis=1), 'expert', split_axis=0...]
    all_gather x2 -> x4, waiting for transfers between devices: 0.02 us -> 142 us  [the longest x1 54.1 us: body(): w_in = lax.all_gather(gate_up, 'dp', axis=1, tiled=True)]
    reduce_scatter x2 -> x5, waiting for transfers between devices: 33.5 us -> 135 us  [the longest x4 99.6 us: scatter(): lax.psum_scatter(full, 'dp', scatter_dimension=0, tiled=True)]
    scatter x3 -> x0, local copies, waits for them, and re-layouts: 21.8 us -> none  [the longest x1 7.59 us: body(): jnp.zeros((buffer_rows,), jnp.bfloat16).at[slot_dest]]
    all_to_all x5 -> x1, starting transfers between devices: 23.5 us -> 3.31 us  [body(): lax.all_to_all(jnp.concatenate(gate_sums, axis=1), 'expert', split_axis=0...]
    dot_general x5 -> x10, matrix products: 27.9 us -> 44.4 us  [the longest x4 17.7 us: scatter(): lax.dot_general(left, right, (((0,), (0,)), ((), ())), preferred_element_...]
    gather x2 -> x0, local copies, waits for them, and re-layouts: 12.1 us -> none  [the longest x1 6.81 us: body(): back_gate.reshape(buffer_rows)[slot_dest].reshape(tok_count, TOP)]
    all_to_all x6 -> x0, local copies, waits for them, and re-layouts: 8.36 us -> none  [the longest x1 3.71 us: body(): lax.all_to_all(send_dy.reshape(block_shape), 'expert', split_axis=0, conc...]
  transfers between devices with their start and end apart: 9 -> 10, of which waited for: 5 -> 9; matrix products, arithmetic and copies ran while one was open for 23% -> 12% of each run, Pallas kernels for 0% -> 0%
where the time goes in v1:
time: 374 us
  waiting for transfers between devices  285 us (76%)
  matrix products  44.4 us (12%)
  between operations  14 us (4%)
  other arithmetic  11.9 us (3%)
  blocking collectives  7.91 us (2%)
  local copies, waits for them, and re-layouts  6.68 us (2%)
  starting transfers between devices  3.85 us (1%)
    reduce_scatter x4, waiting for transfers between devices, scatter(): lax.psum_scatter(full, 'dp', scatter_dimension=0, tiled=True)  99.6 us
    all_gather x1, waiting for transfers between devices, body(): w_in = lax.all_gather(gate_up, 'dp', axis=1, tiled=True)  54.1 us
    reduce_scatter x1, waiting for transfers between devices, body(): lax.psum_scatter(dx, 'expert', scatter_dimension=0, tiled=True)  35.5 us
    all_gather x1, waiting for transfers between devices, body(): all_x = lax.all_gather(tokens, 'expert', axis=0, tiled=True)  31.5 us
    all_gather x1, waiting for transfers between devices, body(): all_dy = lax.all_gather(cotangent, 'expert', axis=0, tiled=True)  30.6 us
    all_gather x1, waiting for transfers between devices, body(): w_out = lax.all_gather(down_proj, 'dp', axis=1, tiled=True)  26.1 us
    dot_general x4, matrix products, scatter(): lax.dot_general(left, right, (((0,), (0,)), ((), ())), preferred_element_...  17.7 us
    dot_general x2, matrix products, body(): pre_act = jnp.dot(all_x, w_in[j], preferred_element_type=jnp.float32)  11.1 us
  transfers between devices with their start and end apart: 10, of which 9 were waited for; matrix products, arithmetic and copies ran while one was open for 12% of the time, Pallas kernels for 0%

profile of v1, /device:TPU:0, one launch (start us, length us, event | category | flops | bytes accessed | tf_op | source)
XLA Modules:
  0.0 374.0 jit_solution(7064183488051705853)
XLA Ops:
  7.2 0.7 all-gather.9.cloned.1.call-update
  7.9 0.7 all-gather.11.cloned.1.call-update
  8.7 0.7 all-gather.7.cloned.1.call-update
  10.0 31.5 %all-gather.9.cloned.1.call-done = bf16[1024,1024]{1,0:T(8,128)(2,1)} async-done(((bf16[128,1024]{1,0:T(8,128)(2,1)}), bf16[1024,1024]{1,0:T(8,128)(2,1)}) %all-gather.9.cloned.1.call-update) | async-done | bytes 2097168 | tf_op jit(solution)/shard_map/all_gather | solution.py:19
  41.4 54.1 %all-gather.11.cloned.1.call-done = bf16[2,1024,1024]{2,1,0:T(8,128)(2,1)} async-done(((bf16[2,256,1024]{2,1,0:T(8,128)(2,1)}), bf16[2,1024,1024]{2,1,0:T(8,128)(2,1)}) %all-gather.11.cloned.1.call-update) | async-done | bytes 4194320 | tf_op jit(solution)/shard_map/all_gather | solution.py:22
  95.5 6.8 %fusion.4 = f32[1024,1024]{0,1:T(8,128)} fusion(bf16[1024,1024]{1,0:T(8,128)(2,1)} %all-gather.9.cloned.1.call-done, bf16[2,1024,1024]{2,1,0:T(8,128)(2,1)} %all-gather.11.cloned.1.call-done), kind=kOutput, calls=%fused_computation.23 | convolution fusion | flops 2147483648 | bytes 8388608 | tf_op jit(solution)/shard_map/dot_general | solution.py:26
  102.3 4.4 %fusion.3 = f32[1024,1024]{0,1:T(8,128)} fusion(bf16[1024,1024]{1,0:T(8,128)(2,1)S(1)} %copy-done.11, bf16[2,1024,1024]{2,1,0:T(8,128)(2,1)S(1)} %copy-done.9), kind=kOutput, calls=%fused_computation.22 | convolution fusion | flops 2147483648 | bytes 8388608 | tf_op jit(solution)/shard_map/dot_general | solution.py:26
  106.7 26.1 %all-gather.7.cloned.1.call-done = bf16[2,512,1024]{2,1,0:T(8,128)(2,1)} async-done(((bf16[2,128,1024]{2,1,0:T(8,128)(2,1)}), bf16[2,512,1024]{2,1,0:T(8,128)(2,1)}) %all-gather.7.cloned.1.call-update) | async-done | bytes 2097168 | tf_op jit(solution)/shard_map/all_gather | solution.py:23
  132.7 30.6 %all-gather.5.cloned.1.call-done = bf16[1024,1024]{1,0:T(8,128)(2,1)} async-done(((bf16[128,1024]{1,0:T(8,128)(2,1)}), bf16[1024,1024]{1,0:T(8,128)(2,1)}) %all-gather.5.cloned.1.call-update) | async-done | bytes 2097168 | tf_op jit(solution)/shard_map/all_gather | solution.py:20
  163.3 4.8 %multiply_reduce_fusion = (bf16[1024]{0:T(1024)(128)(2,1)S(1)}, f32[1024,512]{0,1:T(8,128)S(1)}) fusion(f32[1024,1024]{0,1:T(8,128)} %fusion.4, bf16[1024,1024]{1,0:T(8,128)(2,1)} %all-gather.5.cloned.1.call-done, bf16[2,512,1024]{2,1,0:T(8,128)(2,1)} %all-gather.7.cloned.1.call-done), kind=kOutput, calls=%fused_computation.9 | convolution fusion | flops 1077410816 | bytes 9439232 | tf_op jit(solution)/shard_map/dot_general | solution.py:31
  168.9 2.7 multiply_reduce_fusion.1
  172.3 3.3 all-to-all-start.1
  175.7 5.3 %all-to-all-done.1 = bf16[8,128,2]{1,2,0:T(2,128)(2,1)S(1)} async-done(((bf16[8,128,2]{1,2,0:T(2,128)(2,1)}), bf16[8,128,2]{1,2,0:T(2,128)(2,1)S(1)}, u32[]{:S(2)}, u32[]{:S(2)}) %all-to-all-start.1) | async-done | bytes 4128 | tf_op jit(solution)/shard_map/all_to_all | solution.py:57
  181.6 7.9 %all_to_all.26 = bf16[128,8,2]{0,2,1:T(2,128)(2,1)S(1)} all-to-all(bf16[128,8,2]{0,2,1:T(2,128)(2,1)S(1)} %bitcast.59), channel_id=1, replica_groups=mesh['dp'=4,'expert'=8] {'expert'}, dimensions={1} | all-to-all | bytes 8192 | tf_op jit(solution)/shard_map/all_to_all | solution.py:21
  189.6 5.2 %convolution_convert_fusion.1 = bf16[512,1024]{1,0:T(8,128)(2,1)} fusion(bf16[1024,1024]{1,0:T(8,128)(2,1)} %all-gather.5.cloned.1.call-done, f32[1024]{0:T(1024)S(1)} %bitcast.57, f32[1024,1024]{0,1:T(8,128)} %fusion.3), kind=kOutput, calls=%fused_computation.25 | convolution fusion | flops 1077936128 | bytes 7344128 | tf_op jit(solution)/shard_map/dot_general | solution.py:43
  194.8 5.2 %convolution_convert_fusion = bf16[512,1024]{1,0:T(8,128)(2,1)} fusion(bf16[1024,1024]{1,0:T(8,128)(2,1)} %all-gather.5.cloned.1.call-done, f32[1024]{0:T(1024)S(1)} %bitcast.55, f32[1024,1024]{0,1:T(8,128)} %fusion.4), kind=kOutput, calls=%fused_computation.24 | convolution fusion | flops 1077936128 | bytes 7344128 | tf_op jit(solution)/shard_map/dot_general | solution.py:43
  200.3 4.2 %multiply_convert_fusion.5 = (bf16[1024,512]{0,1:T(8,128)(2,1)S(1)}, bf16[1024,512]{0,1:T(8,128)(2,1)S(1)}) fusion(f32[1024,1024]{0,1:T(8,128)} %fusion.3, f32[1024,512]{0,1:T(8,128)} %get-tuple-element.31, f32[1024]{0:T(1024)S(1)} %bitcast.58), kind=kLoop, calls=%fused_computation.16 | loop fusion | flops 7340032 | bytes 8392704 | tf_op jit(solution)/shard_map/convert.12
  204.5 1.0 copy-done.1
  205.5 3.7 convert_bitcast_fusion.1
  209.3 3.6 multiply_convert_fusion.3
  212.9 1.0 copy-done.3
  214.2 3.7 convert_bitcast_fusion
  218.0 1.1 copy-done.2
  219.1 4.2 %fusion.2 = f32[1024,1024]{1,0:T(8,128)S(1)} fusion(bf16[2,1024,1024]{2,1,0:T(8,128)(2,1)} %all-gather.11.cloned.1.call-done, bf16[1024,512]{0,1:T(8,128)(2,1)S(1)} %copy-done.2, bf16[1024,512]{0,1:T(8,128)(2,1)S(1)} %get-tuple-element.24), kind=kOutput, calls=%fused_computation.21 | convolution fusion | flops 2151677952 | bytes 8388608 | tf_op jit(solution)/shard_map/dot_general | solution.py:51
  223.3 3.8 %add_convert_fusion = bf16[1024,1024]{1,0:T(8,128)(2,1)} fusion(f32[1024,1024]{1,0:T(8,128)S(1)} %fusion.2, bf16[2,1024,1024]{2,1,0:T(8,128)(2,1)S(1)} %copy-done.10, bf16[1024,512]{0,1:T(8,128)(2,1)S(1)} %copy-done.6, bf16[1024,512]{0,1:T(8,128)(2,1)S(1)} %copy-done.4), kind=kOutput, calls=%fused_computation | convolution fusion | flops 2153775104 | bytes 10485760 | tf_op jit(solution)/shard_map/dot_general | solution.py:51
  227.1 24.5 %reduce-scatter.14.cloned.1.call-done = bf16[128,1024]{1,0:T(8,128)(2,1)} async-done(((bf16[512,1024]{1,0:T(8,128)(2,1)}), bf16[128,1024]{1,0:T(8,128)(2,1)}) %reduce-scatter.14.cloned.1.call-update) | async-done | bytes 262160 | tf_op jit(solution)/shard_map/reduce_scatter | solution.py:46
  251.6 2.1 maximum_convert_fusion.1
  253.7 36.1 %reduce-scatter.8.cloned.1.call-done = bf16[256,1024]{0,1:T(8,128)(2,1)} async-done(((bf16[1024,1024]{0,1:T(8,128)(2,1)}), bf16[256,1024]{0,1:T(8,128)(2,1)}) %reduce-scatter.8.cloned.1.call-update) | async-done | bytes 524304 | tf_op jit(solution)/shard_map/reduce_scatter | solution.py:46
  289.8 39.0 %reduce-scatter.10.cloned.1.call-done = bf16[256,1024]{0,1:T(8,128)(2,1)} async-done(((bf16[1024,1024]{0,1:T(8,128)(2,1)}), bf16[256,1024]{0,1:T(8,128)(2,1)}) %reduce-scatter.10.cloned.1.call-update) | async-done | bytes 524304 | tf_op jit(solution)/shard_map/reduce_scatter | solution.py:46
  328.8 1.3 maximum_convert_fusion
  330.1 1.8 copy.24
  332.0 35.5 %reduce-scatter.6.cloned.1.call-done = bf16[128,1024]{1,0:T(8,128)(2,1)} async-done(((bf16[1024,1024]{1,0:T(8,128)(2,1)}), bf16[128,1024]{1,0:T(8,128)(2,1)}) %reduce-scatter.6.cloned.1.call-update) | async-done | bytes 262160 | tf_op jit(solution)/shard_map/reduce_scatter | solution.py:56
  (51 shorter events, 3.6 us)
Async XLA Ops:
  7.2 34.3 %all-gather.9.cloned.1.call-start = ((), (), s32[]{:S(2)}) async-start(), calls=%async_computation.9 | async-start | bytes 2359296 | tf_op jit(solution)/shard_map/all_gather | solution.py:19
  7.9 87.6 %all-gather.11.cloned.1.call-start = ((), (), s32[]{:S(2)}) async-start(), calls=%async_computation.10 | async-start | bytes 5242880 | tf_op jit(solution)/shard_map/all_gather | solution.py:22
  8.6 124.1 %all-gather.7.cloned.1.call-start = ((), (), s32[]{:S(2)}) async-start(), calls=%async_computation.8 | async-start | bytes 2621440 | tf_op jit(solution)/shard_map/all_gather | solution.py:23
  9.4 153.9 %all-gather.5.cloned.1.call-start = ((), (), s32[]{:S(2)}) async-start(), calls=%async_computation.7 | async-start | bytes 2359296 | tf_op jit(solution)/shard_map/all_gather | solution.py:20
  41.4 60.8 %copy-start.11 = (bf16[1024,1024]{1,0:T(8,128)(2,1)S(1)}, bf16[1024,1024]{1,0:T(8,128)(2,1)}, u32[]{:S(2)}) copy-start(bf16[1024,1024]{1,0:T(8,128)(2,1)} %all-gather.9.cloned.1.call-done) | copy-start | bytes 6291460
  95.5 6.8 %copy-start.9 = (bf16[2,1024,1024]{2,1,0:T(8,128)(2,1)S(1)}, bf16[2,1024,1024]{2,1,0:T(8,128)(2,1)}, u32[]{:S(2)}) copy-start(bf16[2,1024,1024]{2,1,0:T(8,128)(2,1)} %all-gather.11.cloned.1.call-done) | copy-start | bytes 12582916
  163.3 4.8 %copy-start = (f32[1024,1024]{0,1:T(8,128)S(1)}, f32[1024,1024]{0,1:T(8,128)}, u32[]{:S(2)}) copy-start(f32[1024,1024]{0,1:T(8,128)} %fusion.3) | copy-start | bytes 12582916
  163.3 5.0 %copy-start.14 = (bf16[1024,1024]{1,0:T(8,128)(2,1)S(1)}, bf16[1024,1024]{1,0:T(8,128)(2,1)}, u32[]{:S(2)}) copy-start(bf16[1024,1024]{1,0:T(8,128)(2,1)} %all-gather.5.cloned.1.call-done) | copy-start | bytes 6291460
  163.3 5.6 %copy-start.15 = (bf16[2,512,1024]{2,1,0:T(8,128)(2,1)S(1)}, bf16[2,512,1024]{2,1,0:T(8,128)(2,1)}, u32[]{:S(2)}) copy-start(bf16[2,512,1024]{2,1,0:T(8,128)(2,1)} %all-gather.7.cloned.1.call-done) | copy-start | bytes 6291460
  168.9 6.7 %copy-start.8 = (bf16[128,8]{0,1:T(8,128)(2,1)S(1)}, bf16[128,8]{0,1:T(8,128)(2,1)}, u32[]{:S(2)}) copy-start(bf16[128,8]{0,1:T(8,128)(2,1)} %param.9) | copy-start | bytes 6148
  168.9 12.1 %copy-start.7 = (s32[128,8]{0,1:T(8,128)S(1)}, s32[128,8]{0,1:T(8,128)}, u32[]{:S(2)}) copy-start(s32[128,8]{0,1:T(8,128)} %param.8) | copy-start | bytes 12292
  172.3 8.7 %all-to-all-start.1 = ((bf16[8,128,2]{1,2,0:T(2,128)(2,1)}), bf16[8,128,2]{1,2,0:T(2,128)(2,1)S(1)}, u32[]{:S(2)}, u32[]{:S(2)}) async-start(bf16[8,128,2]{1,2,0:T(2,128)(2,1)} %copy.23), calls=%async_computation.2 | async-start | bytes 8192 | tf_op jit(solution)/shard_map/all_to_all | solution.py:57
  175.6 51.5 %reduce-scatter.12.cloned.1.call-start = ((), (), s32[]{:S(2)}) async-start(), calls=%async_computation.14 | async-start | bytes 1310720 | tf_op jit(solution)/shard_map/reduce_scatter | solution.py:46
  194.8 56.8 %reduce-scatter.14.cloned.1.call-start = ((), (), s32[]{:S(2)}) async-start(), calls=%async_computation.15 | async-start | bytes 1310720 | tf_op jit(solution)/shard_map/reduce_scatter | solution.py:46
  200.0 89.8 %reduce-scatter.8.cloned.1.call-start = ((), (), s32[]{:S(2)}) async-start(), calls=%async_computation.12 | async-start | bytes 2621440 | tf_op jit(solution)/shard_map/reduce_scatter | solution.py:46
  200.2 5.2 %copy-start.12 = (bf16[1024,1024]{1,0:T(8,128)(2,1)S(1)}, bf16[1024,1024]{1,0:T(8,128)(2,1)}, u32[]{:S(2)}) copy-start(bf16[1024,1024]{1,0:T(8,128)(2,1)} %all-gather.9.cloned.1.call-done) | copy-start | bytes 6291460
  204.5 1.0 copy-start.1
  209.2 119.6 %reduce-scatter.10.cloned.1.call-start = ((), (), s32[]{:S(2)}) async-start(), calls=%async_computation.13 | async-start | bytes 2621440 | tf_op jit(solution)/shard_map/reduce_scatter | solution.py:46
  209.3 5.0 %copy-start.13 = (bf16[1024,1024]{1,0:T(8,128)(2,1)S(1)}, bf16[1024,1024]{1,0:T(8,128)(2,1)}, u32[]{:S(2)}) copy-start(bf16[1024,1024]{1,0:T(8,128)(2,1)} %all-gather.9.cloned.1.call-done) | copy-start | bytes 6291460
  212.9 1.0 copy-start.3
  212.9 1.3 copy-start.5
  217.9 1.2 copy-start.2
  217.9 5.4 %copy-start.4 = (bf16[1024,512]{0,1:T(8,128)(2,1)S(1)}, bf16[1024,512]{0,1:T(8,128)(2,1)}, u32[]{:S(2)}) copy-start(bf16[1024,512]{0,1:T(8,128)(2,1)} %copy-done.3) | copy-start | bytes 3145732
  217.9 149.5 %reduce-scatter.6.cloned.1.call-start = ((), (), s32[]{:S(2)}) async-start(), calls=%async_computation.11 | async-start | bytes 2359296 | tf_op jit(solution)/shard_map/reduce_scatter | solution.py:56
  219.1 4.2 %copy-start.6 = (bf16[1024,512]{0,1:T(8,128)(2,1)S(1)}, bf16[1024,512]{0,1:T(8,128)(2,1)}, u32[]{:S(2)}) copy-start(bf16[1024,512]{0,1:T(8,128)(2,1)} %copy-done.5) | copy-start | bytes 3145732
  219.1 4.2 %copy-start.10 = (bf16[2,1024,1024]{2,1,0:T(8,128)(2,1)S(1)}, bf16[2,1024,1024]{2,1,0:T(8,128)(2,1)}, u32[]{:S(2)}) copy-start(bf16[2,1024,1024]{2,1,0:T(8,128)(2,1)} %all-gather.11.cloned.1.call-done) | copy-start | bytes 12582916
Sparse Core Ops, SparseCore 0:
  9.6 31.7 all-gather.8
  43.3 52.1 all-gather.10
  97.4 35.3 all-gather.6
  134.2 29.0 all-gather.4
  194.9 25.8 reduce-scatter.11
  223.8 27.7 reduce-scatter.13
  254.6 35.1 reduce-scatter.7
  293.6 35.1 reduce-scatter.9
  331.7 35.7 reduce-scatter.5

commit v2 on v1

v2 whole, which is shorter than its diff:
```python
import functools
import math

import jax
import jax.numpy as jnp
from jax import lax
from jax.experimental import pallas as pl
from jax.experimental.pallas import tpu as pltpu
from jax.sharding import PartitionSpec as P

EXP_DEV = 2
LANES = 128
BF16 = jnp.bfloat16
F32 = jnp.float32


def dot(a, b):
    return jnp.dot(a, b, preferred_element_type=F32)


def dot_nt(a, b):
    return lax.dot_general(a, b, (((1,), (1,)), ((), ())), preferred_element_type=F32)


def kernel(
    ny, nx, nz,
    x_ref, dy_ref, ids_ref, gates_ref, wgu_ref, wd_ref,
    gtok_ref, ggate_ref, ggu_ref, gd_ref,
    blocks, x_t, w_in, w_out, pre, act_t, g_in, g_out,
    in_r1a, in_r1b, in_r2a, in_r2b, out_r1a, out_r1b, out_r2a, out_r2b,
    dxp, dx_r1, dx_r2,
    send_sems, recv_sems, up_sems, down_sems, side_sems, chain_sems, pair_sems,
):
    dp, me = lax.axis_index("dp"), lax.axis_index("expert")
    y, x = dp // nx, dp % nx
    z, c = me // 2, me % 2
    tok, width = x_ref.shape
    rows_in, cols_in = wgu_ref.shape[1:]
    rows_out = wd_ref.shape[1]
    half_in, half_out = rows_in // 2, rows_out // 2
    hidden = cols_in // 2
    total = nz * 2 * tok
    top = ids_ref.shape[1]

    def on_y(o):
        return (lax.rem(y + o, ny) * nx + x, me)

    def on_x(o):
        return (y * nx + lax.rem(x + o, nx), me)

    def on_z(zz):
        return (dp, zz * 2 + c)

    partner = (dp, z * 2 + 1 - c)
    peers = [on_y(o) for o in range(1, ny)] + [on_x(o) for o in range(1, nx)]
    peers += [on_z(lax.rem(z + o, nz)) for o in range(1, nz)] + [partner]

    barrier = pltpu.get_barrier_semaphore()
    for peer in peers:
        pl.semaphore_signal(barrier, inc=1, device_id=peer, device_id_type=pl.DeviceIdType.MESH)

    lane = lax.broadcasted_iota(jnp.int32, (tok, LANES), 1)
    dense = jnp.zeros((tok, LANES), F32)
    for k in range(top):
        dense += jnp.where(ids_ref[:, k : k + 1] == lane, gates_ref[:, k : k + 1].astype(F32), 0.0)
    blocks[z, c, :, :width] = x_ref[...]
    blocks[z, c, :, width : 2 * width] = dy_ref[...]
    blocks[z, c, :, 2 * width :] = dense.astype(BF16)
    for j in range(EXP_DEV):
        w_in[j, y, x] = wgu_ref[j].reshape(2, half_in, cols_in)
        w_out[j, y, x] = wd_ref[j].reshape(2, half_out, width)

    pl.semaphore_wait(barrier, len(peers))

    started = []

    def push(src, dst, peer):
        i = len(started)
        copy = pltpu.make_async_remote_copy(
            src_ref=src, dst_ref=dst, send_sem=send_sems.at[i], recv_sem=recv_sems.at[i],
            device_id=peer, device_id_type=pl.DeviceIdType.MESH,
        )
        copy.start()
        started.append(copy)
        return copy

    def arrived(copies):
        for copy in copies:
            copy.wait_recv()

    def block_copy(origin, send_sem, recv_sem, peer):
        ref = blocks.at[origin, c]
        return pltpu.make_async_remote_copy(
            src_ref=ref, dst_ref=ref, send_sem=send_sem, recv_sem=recv_sem,
            device_id=peer, device_id_type=pl.DeviceIdType.MESH,
        )

    def up(origin):
        peer = on_z(jnp.minimum(z + 1, nz - 1))
        return block_copy(origin, up_sems.at[origin], chain_sems.at[origin], peer)

    def down(origin):
        peer = on_z(jnp.maximum(z - 1, 0))
        return block_copy(origin, down_sems.at[origin], chain_sems.at[origin], peer)

    def side(origin):
        return block_copy(origin, side_sems.at[origin], pair_sems.at[origin], partner)

    def transpose(zz, cc):
        at = pl.multiple_of((zz * 2 + cc) * tok, tok)
        x_t[:, pl.ds(at, tok)] = blocks[zz, cc, :, :width].T

    def chain_step(s):
        @pl.when(z - s >= 0)
        def _():
            origin = z - s
            up(origin).wait_recv()

            @pl.when(z < nz - 1)
            def _():
                up(origin).start()

            side(origin).start()
            transpose(origin, c)

        @pl.when(z + s < nz)
        def _():
            origin = z + s
            down(origin).wait_recv()

            @pl.when(z > 0)
            def _():
                down(origin).start()

            side(origin).start()
            transpose(origin, c)

    def weights_first(j):
        copies = []
        for o in range(1, nx):
            for w in (w_in, w_out):
                copies.append(push(w.at[j, y, x, 0], w.at[j, y, x, 0], on_x(o)))
        for o in range(1, ny):
            for w in (w_in, w_out):
                copies.append(push(w.at[j, y, x, 1], w.at[j, y, x, 1], on_y(o)))
        return copies

    def weights_second(j):
        copies = []
        for o in range(1, ny):
            for w in (w_in, w_out):
                copies.append(push(w.at[j, y, :, 0], w.at[j, y, :, 0], on_y(o)))
        for o in range(1, nx):
            for w in (w_in, w_out):
                copies.append(push(w.at[j, :, x, 1], w.at[j, :, x, 1], on_x(o)))
        return copies

    first0 = weights_first(0)

    @pl.when(z < nz - 1)
    def _():
        up(z).start()

    @pl.when(z > 0)
    def _():
        down(z).start()

    side(z).start()
    transpose(z, c)
    arrived(first0)
    second0 = weights_second(0)
    first1 = weights_first(1)
    for s in range(1, nz - 1):
        chain_step(s)
    arrived(first1)
    second1 = weights_second(1)
    chain_step(nz - 1)

    for zz in range(nz):
        side(zz).wait_recv()
        transpose(zz, 1 - c)

    group = min(nz, max(1, 512 // (2 * tok)))
    rows = group * 2 * tok
    glane = lax.broadcasted_iota(jnp.int32, (rows, LANES), 1)

    def forward(j):
        def step(i, carry):
            at = pl.ds(i * group, group)
            gates = blocks[at, :, :, 2 * width :].reshape(rows, LANES).astype(F32)
            mine = glane == EXP_DEV * me + j
            g = jnp.sum(jnp.where(mine, gates, 0.0), axis=1, keepdims=True)
            pre_act = dot(
                blocks[at, :, :, :width].reshape(rows, width), w_in[j].reshape(width, cols_in)
            )
            raw = dot_nt(
                blocks[at, :, :, width : 2 * width].reshape(rows, width),
                w_out[j].reshape(hidden, width),
            )
            gate_pre, up_pre = pre_act[:, :hidden], pre_act[:, hidden:]
            sig = jax.nn.sigmoid(gate_pre)
            silu = gate_pre * sig
            act = silu * up_pre
            act_grad = g * raw
            r = pl.ds(pl.multiple_of(i * rows, rows), rows)
            pre[j, r, :hidden] = (act_grad * up_pre * sig * (1.0 + gate_pre * (1.0 - sig))).astype(BF16)
            pre[j, r, hidden:] = (act_grad * silu).astype(BF16)
            act_t[:, r] = (g * act).astype(BF16).T
            sums = jnp.sum(act * raw, axis=1, keepdims=True)
            placed = jnp.where(mine, sums, 0.0)
            if j > 0:
                placed += dxp[at, :, :, width:].reshape(rows, LANES).astype(F32)
            dxp[at, :, :, width:] = placed.astype(BF16).reshape(group, 2, tok, LANES)
            return carry

        lax.fori_loop(0, nz // group, step, 0)

    def gradients(j):
        def step(yy, carry):
            r_in, r_out = nx * rows_in, nx * rows_out
            part = dot(x_t[pl.ds(pl.multiple_of(yy * r_in, r_in), r_in), :], pre[j])
            g_in[j, yy] = part.astype(BF16).reshape(nx, 2, half_in, cols_in)
            part = dot(
                act_t[pl.ds(pl.multiple_of(yy * r_out, r_out), r_out), :],
                blocks[:, :, :, width : 2 * width].reshape(total, width),
            )
            g_out[j, yy] = part.astype(BF16).reshape(nx, 2, half_out, width)
            return carry

        lax.fori_loop(0, ny, step, 0)

    kinds = (
        (g_in, in_r1a, in_r1b, in_r2a, in_r2b, ggu_ref, half_in),
        (g_out, out_r1a, out_r1b, out_r2a, out_r2b, gd_ref, half_out),
    )

    def sums_first(j):
        copies = []
        for grad, r1a, r1b, _, _, _, _ in kinds:
            for o in range(1, ny):
                to = lax.rem(y + o, ny)
                copies.append(push(grad.at[j, to, :, 0], r1a.at[j, o - 1], on_y(o)))
            for o in range(1, nx):
                to = lax.rem(x + o, nx)
                copies.append(push(grad.at[j, :, to, 1], r1b.at[j, o - 1], on_x(o)))
        return copies

    def sums_second(j):
        copies = []
        for grad, r1a, r1b, r2a, r2b, out, half in kinds:
            for o in range(nx):
                to = lax.rem(x + o, nx)
                value = grad[j, y, to, 0].astype(F32)
                for n in range(ny - 1):
                    value += r1a[j, n, to].astype(F32)
                if o == 0:
                    out[j, :half] = value
                else:
                    grad[j, y, to, 0] = value.astype(BF16)
                    copies.append(push(grad.at[j, y, to, 0], r2a.at[j, o - 1], on_x(o)))
            for o in range(ny):
                to = lax.rem(y + o, ny)
                value = grad[j, to, x, 1].astype(F32)
                for n in range(nx - 1):
                    value += r1b[j, n, to].astype(F32)
                if o == 0:
                    out[j, half:] = value
                else:
                    grad[j, to, x, 1] = value.astype(BF16)
                    copies.append(push(grad.at[j, to, x, 1], r2b.at[j, o - 1], on_y(o)))
        return copies

    def sums_last(j):
        for _, _, _, r2a, r2b, out, half in kinds:
            value = out[j, :half]
            for n in range(nx - 1):
                value += r2a[j, n].astype(F32)
            out[j, :half] = value
            value = out[j, half:]
            for n in range(ny - 1):
                value += r2b[j, n].astype(F32)
            out[j, half:] = value

    arrived(second0)
    forward(0)
    gradients(0)
    sums0 = sums_first(0)
    arrived(second1)
    forward(1)
    gradients(1)
    arrived(sums0)
    last0 = sums_second(0)
    sums1 = sums_first(1)

    def dx_step(i, carry):
        r = pl.ds(pl.multiple_of(i * rows, rows), rows)
        value = dot_nt(pre[0, r, :], w_in[0].reshape(width, cols_in))
        value += dot_nt(pre[1, r, :], w_in[1].reshape(width, cols_in))
        at = pl.ds(i * group, group)
        dxp[at, :, :, :width] = value.astype(BF16).reshape(group, 2, tok, width)
        return carry

    lax.fori_loop(0, nz // group, dx_step, 0)
    pair = push(dxp.at[:, 1 - c], dx_r1, partner)
    arrived([pair])
    spread = []
    for o in range(1, nz):
        to = lax.rem(z + o, nz)
        dxp[to, c] = (dxp[to, c].astype(F32) + dx_r1[to].astype(F32)).astype(BF16)
        spread.append(push(dxp.at[to, c], dx_r2.at[o - 1], on_z(to)))

    arrived(last0)
    sums_last(0)
    arrived(sums1)
    last1 = sums_second(1)

    arrived(spread)
    value = dxp[z, c].astype(F32) + dx_r1[z].astype(F32)
    for n in range(nz - 1):
        value += dx_r2[n].astype(F32)
    gtok_ref[...] = value[:, :width].astype(BF16)
    back = value[:, width:]
    picked = jnp.zeros((tok, LANES), F32)
    for k in range(top):
        one = jnp.sum(jnp.where(ids_ref[:, k : k + 1] == lane, back, 0.0), axis=1, keepdims=True)
        picked += jnp.where(lane == k, one, 0.0)
    ggate_ref[...] = picked[:, :top].astype(BF16)

    arrived(last1)
    sums_last(1)

    for copy in started:
        copy.wait_send()

    def drain(origin):
        side(origin).wait_send()

        @pl.when((origin <= z) & (z < nz - 1))
        def _():
            up(origin).wait_send()

        @pl.when((origin >= z) & (z > 0))
        def _():
            down(origin).wait_send()

    for zz in range(nz):
        drain(zz)


def body(ny, nx, nz, tokens, cotangent, expert_ids, gate_probs, gate_up, down_proj):
    tok, width = tokens.shape
    rows_in, cols_in = gate_up.shape[1:]
    rows_out = down_proj.shape[1]
    hi, ho = rows_in // 2, rows_out // 2
    total = nz * 2 * tok
    copies = 16 * (nx + ny - 2) + nz
    V = pltpu.VMEM
    dma = pltpu.SemaphoreType.DMA
    e = EXP_DEV
    flops = 2 * e * total * width * cols_in * 4
    return pl.pallas_call(
        functools.partial(kernel, ny, nx, nz),
        out_shape=(
            jax.ShapeDtypeStruct(tokens.shape, BF16),
            jax.ShapeDtypeStruct(gate_probs.shape, BF16),
            jax.ShapeDtypeStruct(gate_up.shape, F32),
            jax.ShapeDtypeStruct(down_proj.shape, F32),
        ),
        in_specs=[pl.BlockSpec(memory_space=V)] * 6,
        out_specs=[pl.BlockSpec(memory_space=V)] * 4,
        scratch_shapes=[
            V((nz, 2, tok, 2 * width + LANES), BF16),
            V((width, total), BF16),
            V((e, ny, nx, 2, hi, cols_in), BF16),
            V((e, ny, nx, 2, ho, width), BF16),
            V((e, total, cols_in), BF16),
            V((cols_in // 2, total), BF16),
            V((e, ny, nx, 2, hi, cols_in), BF16),
            V((e, ny, nx, 2, ho, width), BF16),
            V((e, ny - 1, nx, hi, cols_in), BF16),
            V((e, nx - 1, ny, hi, cols_in), BF16),
            V((e, nx - 1, hi, cols_in), BF16),
            V((e, ny - 1, hi, cols_in), BF16),
            V((e, ny - 1, nx, ho, width), BF16),
            V((e, nx - 1, ny, ho, width), BF16),
            V((e, nx - 1, ho, width), BF16),
            V((e, ny - 1, ho, width), BF16),
            V((nz, 2, tok, width + LANES), BF16),
            V((nz, tok, width + LANES), BF16),
            V((nz - 1, tok, width + LANES), BF16),
            dma((copies,)),
            dma((copies,)),
            dma((nz,)),
            dma((nz,)),
            dma((nz,)),
            dma((nz,)),
            dma((nz,)),
        ],
        compiler_params=pltpu.CompilerParams(
            collective_id=0, has_side_effects=True, vmem_limit_bytes=60 * 2**20
        ),
        cost_estimate=pl.CostEstimate(flops=flops, bytes_accessed=8 * 2**20, transcendentals=0),
    )(tokens, cotangent, expert_ids, gate_probs, gate_up, down_proj)


def solution(mesh):
    dp = mesh.shape["dp"]
    nx = next(n for n in range(math.isqrt(dp), 0, -1) if dp % n == 0)
    tok = P(("dp", "expert"), None)
    wgt = P("expert", "dp", None)
    return jax.shard_map(
        functools.partial(body, dp // nx, nx, mesh.shape["expert"] // 2),
        mesh=mesh,
        in_specs=(tok, tok, tok, tok, wgt, wgt),
        out_specs=(tok, tok, wgt, wgt),
        check_vma=False,
    )
```

time: 374 us -> 125 us (0.33)
  waiting for transfers between devices: 285 us -> 0 us
  Pallas kernels: 0 us -> 114 us
  matrix products: 44.4 us -> 0 us
  between operations: 14 us -> 0.64 us
  other arithmetic: 11.9 us -> 0 us
  blocking collectives: 7.91 us -> 0 us
  starting transfers between devices: 3.85 us -> 0 us
    all_gather x4 -> x0, waiting for transfers between devices: 142 us -> none  [the longest x1 54.1 us: body(): w_in = lax.all_gather(gate_up, 'dp', axis=1, tiled=True)]
    reduce_scatter x5 -> x0, waiting for transfers between devices: 135 us -> none  [the longest x4 99.6 us: scatter(): lax.psum_scatter(full, 'dp', scatter_dimension=0, tiled=True)]
    pallas_call x0 -> x1, Pallas kernels: none -> 114 us  [body(): pl.pallas_call(functools.partial(kernel, ny, nx, nz), out_shape=(jax.Shap...]
    dot_general x10 -> x0, matrix products: 44.4 us -> none  [the longest x4 17.7 us: scatter(): lax.dot_general(left, right, (((0,), (0,)), ((), ())), preferred_element_...]
    another operation x4 -> x0, other arithmetic: 11.2 us -> none
    all_to_all x1 -> x0, blocking collectives: 7.91 us -> none  [body(): lax.all_to_all(dense, 'expert', split_axis=1, concat_axis=0, tiled=True)]
    all_to_all x1 -> x0, waiting for transfers between devices: 5.34 us -> none  [body(): lax.all_to_all(jnp.concatenate(gate_sums, axis=1), 'expert', split_axis=0...]
    unnamed x33 -> x7, local copies, waits for them, and re-layouts: 6.08 us -> 8.7 us
  transfers between devices with their start and end apart: 10 -> 0, of which waited for: 9 -> 0; matrix products, arithmetic and copies ran while one was open for 12% -> 0% of each run, Pallas kernels for 0% -> 0%
where the time goes in v2:
time: 125 us; the launch traced here: 124 us
  Pallas kernels  114 us (91%)
  local copies, waits for them, and re-layouts  10.1 us (8%)
    pallas_call x1, Pallas kernels, body(): pl.pallas_call(functools.partial(kernel, ny, nx, nz), out_shape=(jax.Shap...  114 us
    unnamed x7, local copies, waits for them, and re-layouts  8.7 us

profile of v2, /device:TPU:0, one launch (start us, length us, event | category | flops | bytes accessed | tf_op | source)
XLA Modules:
  0.0 124.5 jit_solution(13843503505992034287)
XLA Ops:
  0.6 1.4 %copy.11.gates_ref = bf16[128,8]{1,0:T(8,128)(2,1)} copy(bf16[128,8]{0,1:T(8,128)(2,1)} %param.9) | data formatting | bytes 4096 | tf_op args[3]
  2.0 1.4 %copy.10.ids_ref = s32[128,8]{1,0:T(8,128)} copy(s32[128,8]{0,1:T(8,128)} %param.8) | data formatting | bytes 8192 | tf_op args[2]
  3.4 113.7 %shard_map.93 = (bf16[128,1024]{1,0:T(8,128)(2,1)}, bf16[128,8]{1,0:T(8,128)(2,1)}, f32[2,256,1024]{2,1,0:T(8,128)}, f32[2,128,1024]{2,1,0:T(8,128)}) custom-call(bf16[128,1024]{1,0:T(8,128)(2,1)} %x_ref.1, bf16[128,1024]{1,0:T(8,128)(2,1)} %dy_ref.1, s32[128,8]{1,0:T(8,128)} %copy.10.ids_ref, bf16[128,8]{1,0:T(8,128)(2,1)} %copy.11.gates_ref, ...), custom_call_target="tpu_custom_call" | custom-call | flops 17179869184 | bytes 8388608 | tf_op jit(solution)/shard_map/pallas_call | solution.py:361
  117.2 1.4 %copy.12 = bf16[128,8]{0,1:T(8,128)(2,1)} copy(bf16[128,8]{1,0:T(8,128)(2,1)} %get-tuple-element.5) | data formatting | bytes 4096 | tf_op jit(solution)/shard_map/pallas_call | solution.py:361
  118.6 1.7 %copy.16 = bf16[128,1024]{1,0:T(8,128)(2,1)} copy(bf16[128,1024]{1,0:T(8,128)(2,1)} %get-tuple-element.12) | data formatting | bytes 524288
  120.2 0.0 copy-start
  120.2 3.2 %copy.17 = f32[2,256,1024]{2,1,0:T(8,128)} copy(f32[2,256,1024]{2,1,0:T(8,128)} %get-tuple-element.14) | data formatting | bytes 4194304
  123.5 0.0 copy-done
  123.5 1.0 copy.18
Async XLA Ops:
  120.2 3.3 %copy-start = (f32[2,128,1024]{2,1,0:T(8,128)S(1)}, f32[2,128,1024]{2,1,0:T(8,128)}, u32[]{:S(2)}) copy-start(f32[2,128,1024]{2,1,0:T(8,128)} %get-tuple-element.15) | copy-start | bytes 3145732

commit v3 on v2

v3 whole, which is shorter than its diff:
```python
import functools
import math

import jax
import jax.numpy as jnp
from jax import lax
from jax.experimental import pallas as pl
from jax.experimental.pallas import tpu as pltpu
from jax.sharding import PartitionSpec as P

EXP_DEV = 2
LANES = 128
BF16 = jnp.bfloat16
F32 = jnp.float32


def dot(a, b):
    return jnp.dot(a, b, preferred_element_type=F32)


def dot_nt(a, b):
    return lax.dot_general(a, b, (((1,), (1,)), ((), ())), preferred_element_type=F32)


def kernel(
    ny, nx, nz,
    x_ref, dy_ref, ids_ref, gates_ref, wgu_ref, wd_ref,
    gtok_ref, ggate_ref, ggu_ref, gd_ref,
    blocks, x_t, w_in, w_out, pre, act_t, g_in, g_out,
    in_r1a, in_r1b, in_r2a, in_r2b, out_r1a, out_r1b, out_r2a, out_r2b,
    dxp, dx_r1, dx_r2,
    send_sems, recv_sems, up_sems, down_sems, side_sems, chain_sems, pair_sems, own_sems,
):
    dp, me = lax.axis_index("dp"), lax.axis_index("expert")
    y, x = dp // nx, dp % nx
    z, c = me // 2, me % 2
    tok, width = x_ref.shape
    half_in, cols_in = wgu_ref.shape[2:]
    half_out = wd_ref.shape[2]
    rows_in, rows_out = 2 * half_in, 2 * half_out
    hidden = cols_in // 2
    total = nz * 2 * tok
    top = ids_ref.shape[0]

    def on_y(o):
        return (lax.rem(y + o, ny) * nx + x, me)

    def on_x(o):
        return (y * nx + lax.rem(x + o, nx), me)

    def on_z(zz):
        return (dp, zz * 2 + c)

    partner = (dp, z * 2 + 1 - c)
    peers = [on_y(o) for o in range(1, ny)] + [on_x(o) for o in range(1, nx)]
    peers += [on_z(lax.rem(z + o, nz)) for o in range(1, nz)] + [partner]

    barrier = pltpu.get_barrier_semaphore()
    for peer in peers:
        pl.semaphore_signal(barrier, inc=1, device_id=peer, device_id_type=pl.DeviceIdType.MESH)

    own = []
    for j in range(EXP_DEV):
        own.append(pltpu.make_async_copy(wgu_ref.at[j], w_in.at[j, y, x], own_sems.at[2 * j]))
        own.append(pltpu.make_async_copy(wd_ref.at[j], w_out.at[j, y, x], own_sems.at[2 * j + 1]))
    for copy in own:
        copy.start()

    expert = lax.broadcasted_iota(jnp.int32, (LANES, tok), 0)
    ids = ids_ref[...]
    gate_rows = gates_ref[...].astype(F32)
    dense = jnp.zeros((LANES, tok), F32)
    for k in range(top):
        dense += jnp.where(ids[k : k + 1] == expert, gate_rows[k : k + 1], 0.0)
    blocks[z, c, :, :width] = x_ref[...]
    blocks[z, c, :, width : 2 * width] = dy_ref[...]
    blocks[z, c, :, 2 * width :] = dense.T.astype(BF16)

    pl.semaphore_wait(barrier, len(peers))

    started = []

    def push(src, dst, peer):
        i = len(started)
        copy = pltpu.make_async_remote_copy(
            src_ref=src, dst_ref=dst, send_sem=send_sems.at[i], recv_sem=recv_sems.at[i],
            device_id=peer, device_id_type=pl.DeviceIdType.MESH,
        )
        copy.start()
        started.append(copy)
        return copy

    def arrived(copies):
        for copy in copies:
            copy.wait_recv()

    def block_copy(origin, send_sem, recv_sem, peer):
        ref = blocks.at[origin, c]
        return pltpu.make_async_remote_copy(
            src_ref=ref, dst_ref=ref, send_sem=send_sem, recv_sem=recv_sem,
            device_id=peer, device_id_type=pl.DeviceIdType.MESH,
        )

    def up(origin):
        peer = on_z(jnp.minimum(z + 1, nz - 1))
        return block_copy(origin, up_sems.at[origin], chain_sems.at[origin], peer)

    def down(origin):
        peer = on_z(jnp.maximum(z - 1, 0))
        return block_copy(origin, down_sems.at[origin], chain_sems.at[origin], peer)

    def side(origin):
        return block_copy(origin, side_sems.at[origin], pair_sems.at[origin], partner)

    def transpose(zz, cc):
        at = pl.multiple_of((zz * 2 + cc) * tok, tok)
        x_t[:, pl.ds(at, tok)] = blocks[zz, cc, :, :width].T

    def chain_step(s):
        @pl.when(z - s >= 0)
        def _():
            origin = z - s
            up(origin).wait_recv()

            @pl.when(z < nz - 1)
            def _():
                up(origin).start()

            side(origin).start()
            transpose(origin, c)

        @pl.when(z + s < nz)
        def _():
            origin = z + s
            down(origin).wait_recv()

            @pl.when(z > 0)
            def _():
                down(origin).start()

            side(origin).start()
            transpose(origin, c)

    def weights_first(j):
        copies = []
        for o in range(1, nx):
            for ref, w in ((wgu_ref, w_in), (wd_ref, w_out)):
                copies.append(push(ref.at[j, 0], w.at[j, y, x, 0], on_x(o)))
        for o in range(1, ny):
            for ref, w in ((wgu_ref, w_in), (wd_ref, w_out)):
                copies.append(push(ref.at[j, 1], w.at[j, y, x, 1], on_y(o)))
        return copies

    def weights_second(j):
        copies = []
        for o in range(1, ny):
            for w in (w_in, w_out):
                copies.append(push(w.at[j, y, :, 0], w.at[j, y, :, 0], on_y(o)))
        for o in range(1, nx):
            for w in (w_in, w_out):
                copies.append(push(w.at[j, :, x, 1], w.at[j, :, x, 1], on_x(o)))
        return copies

    first0 = weights_first(0)

    @pl.when(z < nz - 1)
    def _():
        up(z).start()

    @pl.when(z > 0)
    def _():
        down(z).start()

    side(z).start()
    transpose(z, c)
    for copy in own:
        copy.wait()
    arrived(first0)
    second0 = weights_second(0)
    first1 = weights_first(1)

    def forward(j, first, group):
        rows = group * 2 * tok
        glane = lax.broadcasted_iota(jnp.int32, (rows, LANES), 1)
        at = pl.ds(first, group)
        gates = blocks[at, :, :, 2 * width :].reshape(rows, LANES).astype(F32)
        mine = glane == EXP_DEV * me + j
        g = jnp.sum(jnp.where(mine, gates, 0.0), axis=1, keepdims=True)
        pre_act = dot(
            blocks[at, :, :, :width].reshape(rows, width), w_in[j].reshape(width, cols_in)
        )
        raw = dot_nt(
            blocks[at, :, :, width : 2 * width].reshape(rows, width),
            w_out[j].reshape(hidden, width),
        )
        gate_pre, up_pre = pre_act[:, :hidden], pre_act[:, hidden:]
        sig = jax.nn.sigmoid(gate_pre)
        silu = gate_pre * sig
        act = silu * up_pre
        act_grad = g * raw
        r = pl.ds(pl.multiple_of(first * (2 * tok), 2 * tok), rows)
        pre[j, r, :hidden] = (act_grad * up_pre * sig * (1.0 + gate_pre * (1.0 - sig))).astype(BF16)
        pre[j, r, hidden:] = (act_grad * silu).astype(BF16)
        act_t[:, r] = (g * act).astype(BF16).T
        sums = jnp.sum(act * raw, axis=1, keepdims=True)
        placed = jnp.where(mine, sums, 0.0)
        if j > 0:
            placed += dxp[at, :, :, width:].reshape(rows, LANES).astype(F32)
        dxp[at, :, :, width:] = placed.astype(BF16).reshape(group, 2, tok, LANES)

    near = jnp.minimum(z, nz - 1 - z)

    def by_distance(n):
        s = (n + 1) // 2
        close = jnp.where(n % 2 == 1, z - s, z + s)
        far = jnp.where(z == near, n, nz - 1 - n)
        return jnp.where(n <= 2 * near, close, far)

    def forward_arrived(n, carry):
        origin = by_distance(n)
        side(origin).wait_recv()
        transpose(origin, 1 - c)
        forward(0, origin, 1)
        return carry

    group = min(nz, max(1, 512 // (2 * tok)))
    rows = group * 2 * tok

    def forward_all(i, carry):
        forward(1, i * group, group)
        return carry

    def gradients_in(j):
        def step(yy, carry):
            r_in = nx * rows_in
            part = dot(x_t[pl.ds(pl.multiple_of(yy * r_in, r_in), r_in), :], pre[j])
            g_in[j, yy] = part.astype(BF16).reshape(nx, 2, half_in, cols_in)
            return carry

        lax.fori_loop(0, ny, step, 0)

    def gradients_out(j):
        def step(yy, carry):
            r_out = nx * rows_out
            part = dot(
                act_t[pl.ds(pl.multiple_of(yy * r_out, r_out), r_out), :],
                blocks[:, :, :, width : 2 * width].reshape(total, width),
            )
            g_out[j, yy] = part.astype(BF16).reshape(nx, 2, half_out, width)
            return carry

        lax.fori_loop(0, ny, step, 0)

    kinds = (
        (g_in, in_r1a, in_r1b, in_r2a, in_r2b, ggu_ref, half_in),
        (g_out, out_r1a, out_r1b, out_r2a, out_r2b, gd_ref, half_out),
    )

    def sums_first(j, kind):
        grad, r1a, r1b = kind[:3]
        along_y, along_x = [], []
        for o in range(1, ny):
            to = lax.rem(y + o, ny)
            along_y.append(push(grad.at[j, to, :, 0], r1a.at[j, o - 1], on_y(o)))
        for o in range(1, nx):
            to = lax.rem(x + o, nx)
            along_x.append(push(grad.at[j, :, to, 1], r1b.at[j, o - 1], on_x(o)))
        return along_y, along_x

    def sums_second(j, kind, firsts):
        grad, r1a, r1b, r2a, r2b, out, half = kind
        along_x, along_y = [], []
        arrived(firsts[0])
        for o in reversed(range(nx)):
            to = lax.rem(x + o, nx)
            value = grad[j, y, to, 0].astype(F32)
            for n in range(ny - 1):
                value += r1a[j, n, to].astype(F32)
            if o == 0:
                out[j, :half] = value
            else:
                grad[j, y, to, 0] = value.astype(BF16)
                along_x.append(push(grad.at[j, y, to, 0], r2a.at[j, o - 1], on_x(o)))
        arrived(firsts[1])
        for o in reversed(range(ny)):
            to = lax.rem(y + o, ny)
            value = grad[j, to, x, 1].astype(F32)
            for n in range(nx - 1):
                value += r1b[j, n, to].astype(F32)
            if o == 0:
                out[j, half:] = value
            else:
                grad[j, to, x, 1] = value.astype(BF16)
                along_y.append(push(grad.at[j, to, x, 1], r2b.at[j, o - 1], on_y(o)))
        return along_x, along_y

    def sums_last(j, kind, seconds):
        r2a, r2b, out, half = kind[3:]
        arrived(seconds[0])
        value = out[j, :half]
        for n in range(nx - 1):
            value += r2a[j, n].astype(F32)
        out[j, :half] = value
        arrived(seconds[1])
        value = out[j, half:]
        for n in range(ny - 1):
            value += r2b[j, n].astype(F32)
        out[j, half:] = value

    for s in range(1, nz - 1):
        chain_step(s)
    arrived(second0)
    lax.fori_loop(0, nz - 1, forward_arrived, 0)
    arrived(first1)
    second1 = weights_second(1)
    chain_step(nz - 1)
    forward_arrived(nz - 1, 0)
    gradients_in(0)
    firsts0 = [sums_first(0, kinds[0])]
    gradients_out(0)
    firsts0.append(sums_first(0, kinds[1]))
    arrived(second1)
    lax.fori_loop(0, nz // group, forward_all, 0)
    gradients_in(1)
    firsts1 = [sums_first(1, kinds[0])]
    gradients_out(1)
    firsts1.append(sums_first(1, kinds[1]))

    def dx_step(i, carry):
        r = pl.ds(pl.multiple_of(i * rows, rows), rows)
        value = dot_nt(pre[0, r, :], w_in[0].reshape(width, cols_in))
        value += dot_nt(pre[1, r, :], w_in[1].reshape(width, cols_in))
        at = pl.ds(i * group, group)
        dxp[at, :, :, :width] = value.astype(BF16).reshape(group, 2, tok, width)
        return carry

    lax.fori_loop(0, nz // group, dx_step, 0)
    pair = push(dxp.at[:, 1 - c], dx_r1, partner)
    seconds0 = [sums_second(0, kind, first) for kind, first in zip(kinds, firsts0)]
    arrived([pair])
    spread = []
    for o in range(1, nz):
        to = lax.rem(z + o, nz)
        dxp[to, c] = (dxp[to, c].astype(F32) + dx_r1[to].astype(F32)).astype(BF16)
        spread.append(push(dxp.at[to, c], dx_r2.at[o - 1], on_z(to)))

    seconds1 = [sums_second(1, kind, first) for kind, first in zip(kinds, firsts1)]
    for kind, second in zip(kinds, seconds0):
        sums_last(0, kind, second)

    arrived(spread)
    value = dxp[z, c].astype(F32) + dx_r1[z].astype(F32)
    for n in range(nz - 1):
        value += dx_r2[n].astype(F32)
    gtok_ref[...] = value[:, :width].astype(BF16)
    back = value[:, width:].T
    for k in range(top):
        ggate_ref[k : k + 1, :] = jnp.sum(
            jnp.where(ids[k : k + 1] == expert, back, 0.0), axis=0, keepdims=True
        )

    for kind, second in zip(kinds, seconds1):
        sums_last(1, kind, second)

    for copy in started:
        copy.wait_send()

    def drain(origin):
        side(origin).wait_send()

        @pl.when((origin <= z) & (z < nz - 1))
        def _():
            up(origin).wait_send()

        @pl.when((origin >= z) & (z > 0))
        def _():
            down(origin).wait_send()

    for zz in range(nz):
        drain(zz)


def emit(gtok, ggu, gd, gtok_out, ggu_out, gd_out, sems):
    copies = [(gtok, gtok_out)]
    for j in range(EXP_DEV):
        for src, dst in ((ggu, ggu_out), (gd, gd_out)):
            half = src.shape[1] // 2
            for h in range(2):
                at = pl.ds(h * half, half)
                copies.append((src.at[j, at], dst.at[j, at]))
    copies = [pltpu.make_async_copy(s, d, sems.at[i]) for i, (s, d) in enumerate(copies)]
    for copy in copies:
        copy.start()
    for copy in copies:
        copy.wait()


def body(ny, nx, nz, tokens, cotangent, expert_ids, gate_probs, gate_up, down_proj):
    tok, width = tokens.shape
    rows_in, cols_in = gate_up.shape[1:]
    rows_out = down_proj.shape[1]
    hi, ho = rows_in // 2, rows_out // 2
    total = nz * 2 * tok
    copies = 16 * (nx + ny - 2) + nz
    V = pltpu.VMEM
    dma = pltpu.SemaphoreType.DMA
    e = EXP_DEV
    flops = 2 * e * total * width * cols_in * 4
    gtok, ggate, ggu, gd = pl.pallas_call(
        functools.partial(kernel, ny, nx, nz),
        out_shape=(
            jax.ShapeDtypeStruct(tokens.shape, BF16),
            jax.ShapeDtypeStruct(gate_probs.shape[::-1], F32),
            jax.ShapeDtypeStruct(gate_up.shape, F32),
            jax.ShapeDtypeStruct(down_proj.shape, F32),
        ),
        in_specs=[pl.BlockSpec(memory_space=V)] * 4 + [pl.BlockSpec(memory_space=pl.ANY)] * 2,
        out_specs=[pl.BlockSpec(memory_space=V)] * 4,
        scratch_shapes=[
            V((nz, 2, tok, 2 * width + LANES), BF16),
            V((width, total), BF16),
            V((e, ny, nx, 2, hi, cols_in), BF16),
            V((e, ny, nx, 2, ho, width), BF16),
            V((e, total, cols_in), BF16),
            V((cols_in // 2, total), BF16),
            V((e, ny, nx, 2, hi, cols_in), BF16),
            V((e, ny, nx, 2, ho, width), BF16),
            V((e, ny - 1, nx, hi, cols_in), BF16),
            V((e, nx - 1, ny, hi, cols_in), BF16),
            V((e, nx - 1, hi, cols_in), BF16),
            V((e, ny - 1, hi, cols_in), BF16),
            V((e, ny - 1, nx, ho, width), BF16),
            V((e, nx - 1, ny, ho, width), BF16),
            V((e, nx - 1, ho, width), BF16),
            V((e, ny - 1, ho, width), BF16),
            V((nz, 2, tok, width + LANES), BF16),
            V((nz, tok, width + LANES), BF16),
            V((nz - 1, tok, width + LANES), BF16),
            dma((copies,)),
            dma((copies,)),
            dma((nz,)),
            dma((nz,)),
            dma((nz,)),
            dma((nz,)),
            dma((nz,)),
            dma((4,)),
        ],
        compiler_params=pltpu.CompilerParams(
            collective_id=0, has_side_effects=True, vmem_limit_bytes=60 * 2**20
        ),
        cost_estimate=pl.CostEstimate(flops=flops, bytes_accessed=8 * 2**20, transcendentals=0),
    )(
        tokens, cotangent, expert_ids.T, gate_probs.T,
        gate_up.reshape(e, 2, hi, cols_in), down_proj.reshape(e, 2, ho, width),
    )
    gtok, ggu, gd = pl.pallas_call(
        emit,
        out_shape=tuple(jax.ShapeDtypeStruct(a.shape, a.dtype) for a in (gtok, ggu, gd)),
        in_specs=[pl.BlockSpec(memory_space=pl.ANY)] * 3,
        out_specs=[pl.BlockSpec(memory_space=pl.ANY)] * 3,
        scratch_shapes=[dma((4 * e + 1,))],
        compiler_params=pltpu.CompilerParams(vmem_limit_bytes=60 * 2**20),
    )(gtok, ggu, gd)
    return gtok, ggate.astype(BF16).T, ggu, gd


def solution(mesh):
    dp = mesh.shape["dp"]
    nx = next(n for n in range(math.isqrt(dp), 0, -1) if dp % n == 0)
    tok = P(("dp", "expert"), None)
    wgt = P("expert", "dp", None)
    return jax.shard_map(
        functools.partial(body, dp // nx, nx, mesh.shape["expert"] // 2),
        mesh=mesh,
        in_specs=(tok, tok, tok, tok, wgt, wgt),
        out_specs=(tok, tok, wgt, wgt),
        check_vma=False,
    )
```

time: 125 us -> 219 us (1.75)
  Pallas kernels: 114 us -> 218 us
  local copies, waits for them, and re-layouts: 10.1 us -> 0.01 us
    pallas_call x0 -> x1, Pallas kernels: none -> 104 us  [body(): pl.pallas_call(emit, out_shape=tuple((jax.ShapeDtypeStruct(a.shape, a.dty...]
    unnamed x7 -> x2, local copies, waits for them, and re-layouts: 8.7 us -> 0.01 us
where the time goes in v3:
time: 219 us
  Pallas kernels  218 us (100%)
    pallas_call x1, Pallas kernels, body(): pl.pallas_call(functools.partial(kernel, ny, nx, nz), out_shape=(jax.Shap...  113 us
    pallas_call x1, Pallas kernels, body(): pl.pallas_call(emit, out_shape=tuple((jax.ShapeDtypeStruct(a.shape, a.dty...  104 us

profile of v3, /device:TPU:0, one launch (start us, length us, event | category | flops | bytes accessed | tf_op | source)
XLA Modules:
  0.0 219.0 jit_solution(4871887312969998499)
XLA Ops:
  0.6 113.4 %shard_map.93 = (bf16[128,1024]{1,0:T(8,128)(2,1)}, f32[8,128]{1,0:T(8,128)}, f32[2,256,1024]{2,1,0:T(8,128)}, f32[2,128,1024]{2,1,0:T(8,128)}) custom-call(bf16[128,1024]{1,0:T(8,128)(2,1)} %x_ref.1, bf16[128,1024]{1,0:T(8,128)(2,1)} %dy_ref.1, s32[8,128]{1,0:T(8,128)} %bitcast.8, bf16[8,128]{1,0:T(8,128)(2,1)} %bitcast.9, ...), custom_call_target="tpu_custom_call" | custom-call | flops 17179869184 | bytes 8388608 | tf_op jit(solution)/shard_map/pallas_call | solution.py:409
  114.0 0.0 copy-start
  114.0 104.4 %shard_map.94 = (bf16[128,1024]{1,0:T(8,128)(2,1)}, f32[2,256,1024]{2,1,0:T(8,128)}, f32[2,128,1024]{2,1,0:T(8,128)}) custom-call(bf16[128,1024]{1,0:T(8,128)(2,1)} %get-tuple-element.11.gtok, f32[2,256,1024]{2,1,0:T(8,128)} %get-tuple-element.12.ggu, f32[2,128,1024]{2,1,0:T(8,128)} %get-tuple-element.13.gd), custom_call_target="tpu_custom_call" | custom-call | tf_op jit(solution)/shard_map/pallas_call | solution.py:456
  218.4 0.0 copy-done
  218.5 0.6 convert_bitcast_fusion
Async XLA Ops:
  114.0 104.4 %copy-start = (f32[8,128]{1,0:T(8,128)S(1)}, f32[8,128]{1,0:T(8,128)}, u32[]{:S(2)}) copy-start(f32[8,128]{1,0:T(8,128)} %get-tuple-element.15) | copy-start | bytes 12292

commit v4 on v3

--- a/solution.py
+++ b/solution.py
@@ -30,6 +30,7 @@
     in_r1a, in_r1b, in_r2a, in_r2b, out_r1a, out_r1b, out_r2a, out_r2b,
     dxp, dx_r1, dx_r2,
     send_sems, recv_sems, up_sems, down_sems, side_sems, chain_sems, pair_sems, own_sems,
+    dxp_send, dxp_recv, dxs_send, dxs_recv,
 ):
     dp, me = lax.axis_index("dp"), lax.axis_index("expert")
     y, x = dp // nx, dp % nx
@@ -144,11 +145,11 @@
     def weights_first(j):
         copies = []
         for o in range(1, nx):
-            for ref, w in ((wgu_ref, w_in), (wd_ref, w_out)):
-                copies.append(push(ref.at[j, 0], w.at[j, y, x, 0], on_x(o)))
+            for w in (w_in, w_out):
+                copies.append(push(w.at[j, y, x, 0], w.at[j, y, x, 0], on_x(o)))
         for o in range(1, ny):
-            for ref, w in ((wgu_ref, w_in), (wd_ref, w_out)):
-                copies.append(push(ref.at[j, 1], w.at[j, y, x, 1], on_y(o)))
+            for w in (w_in, w_out):
+                copies.append(push(w.at[j, y, x, 1], w.at[j, y, x, 1], on_y(o)))
         return copies
 
     def weights_second(j):
@@ -161,6 +162,8 @@
                 copies.append(push(w.at[j, :, x, 1], w.at[j, :, x, 1], on_x(o)))
         return copies
 
+    for copy in own:
+        copy.wait()
     first0 = weights_first(0)
 
     @pl.when(z < nz - 1)
@@ -173,11 +176,8 @@
 
     side(z).start()
     transpose(z, c)
-    for copy in own:
-        copy.wait()
     arrived(first0)
     second0 = weights_second(0)
-    first1 = weights_first(1)
 
     def forward(j, first, group):
         rows = group * 2 * tok
@@ -310,6 +310,7 @@
     for s in range(1, nz - 1):
         chain_step(s)
     arrived(second0)
+    first1 = weights_first(1)
     lax.fori_loop(0, nz - 1, forward_arrived, 0)
     arrived(first1)
     second1 = weights_second(1)
@@ -326,32 +327,49 @@
     gradients_out(1)
     firsts1.append(sums_first(1, kinds[1]))
 
+    def dx_pair(to):
+        return pltpu.make_async_remote_copy(
+            src_ref=dxp.at[to, 1 - c], dst_ref=dx_r1.at[to],
+            send_sem=dxp_send.at[to], recv_sem=dxp_recv.at[to],
+            device_id=partner, device_id_type=pl.DeviceIdType.MESH,
+        )
+
+    def dx_spread(to, slot):
+        return pltpu.make_async_remote_copy(
+            src_ref=dxp.at[to, c], dst_ref=dx_r2.at[slot],
+            send_sem=dxs_send.at[to], recv_sem=dxs_recv.at[slot],
+            device_id=on_z(to), device_id_type=pl.DeviceIdType.MESH,
+        )
+
     def dx_step(i, carry):
-        r = pl.ds(pl.multiple_of(i * rows, rows), rows)
+        to = lax.rem(z + 1 + i, nz)
+        r = pl.ds(pl.multiple_of(to * (2 * tok), 2 * tok), 2 * tok)
         value = dot_nt(pre[0, r, :], w_in[0].reshape(width, cols_in))
         value += dot_nt(pre[1, r, :], w_in[1].reshape(width, cols_in))
-        at = pl.ds(i * group, group)
-        dxp[at, :, :, :width] = value.astype(BF16).reshape(group, 2, tok, width)
+        dxp[to, :, :, :width] = value.astype(BF16).reshape(2, tok, width)
+        dx_pair(to).start()
+
+        @pl.when(i > 0)
+        def _():
+            last = lax.rem(z + i, nz)
+            dx_pair(last).wait_recv()
+            dxp[last, c] = (dxp[last, c].astype(F32) + dx_r1[last].astype(F32)).astype(BF16)
+            dx_spread(last, z).start()
+
         return carry
 
-    lax.fori_loop(0, nz // group, dx_step, 0)
-    pair = push(dxp.at[:, 1 - c], dx_r1, partner)
+    lax.fori_loop(0, nz, dx_step, 0)
     seconds0 = [sums_second(0, kind, first) for kind, first in zip(kinds, firsts0)]
-    arrived([pair])
-    spread = []
-    for o in range(1, nz):
-        to = lax.rem(z + o, nz)
-        dxp[to, c] = (dxp[to, c].astype(F32) + dx_r1[to].astype(F32)).astype(BF16)
-        spread.append(push(dxp.at[to, c], dx_r2.at[o - 1], on_z(to)))
-
     seconds1 = [sums_second(1, kind, first) for kind, first in zip(kinds, firsts1)]
     for kind, second in zip(kinds, seconds0):
         sums_last(0, kind, second)
 
-    arrived(spread)
+    dx_pair(z).wait_recv()
     value = dxp[z, c].astype(F32) + dx_r1[z].astype(F32)
-    for n in range(nz - 1):
-        value += dx_r2[n].astype(F32)
+    for o in range(1, nz):
+        source = lax.rem(z + o, nz)
+        dx_spread(source, source).wait_recv()
+        value += dx_r2[source].astype(F32)
     gtok_ref[...] = value[:, :width].astype(BF16)
     back = value[:, width:].T
     for k in range(top):
@@ -367,6 +385,11 @@
 
     def drain(origin):
         side(origin).wait_send()
+        dx_pair(origin).wait_send()
+
+        @pl.when(origin != z)
+        def _():
+            dx_spread(origin, z).wait_send()
 
         @pl.when((origin <= z) & (z < nz - 1))
         def _():
@@ -380,18 +403,22 @@
         drain(zz)
 
 
-def emit(gtok, ggu, gd, gtok_out, ggu_out, gd_out, sems):
-    copies = [(gtok, gtok_out)]
+def emit(gtok, ggu, gd, gtok_out, ggu_out, gd_out, gtok_v, ggu_v, gd_v, sems_in, sems_out):
+    parts = [(gtok, gtok_v, gtok_out)]
     for j in range(EXP_DEV):
-        for src, dst in ((ggu, ggu_out), (gd, gd_out)):
+        for src, mid, dst in ((ggu, ggu_v, ggu_out), (gd, gd_v, gd_out)):
             half = src.shape[1] // 2
             for h in range(2):
                 at = pl.ds(h * half, half)
-                copies.append((src.at[j, at], dst.at[j, at]))
-    copies = [pltpu.make_async_copy(s, d, sems.at[i]) for i, (s, d) in enumerate(copies)]
-    for copy in copies:
+                parts.append((src.at[j, at], mid.at[j, at], dst.at[j, at]))
+    ins = [pltpu.make_async_copy(s, m, sems_in.at[i]) for i, (s, m, _) in enumerate(parts)]
+    outs = [pltpu.make_async_copy(m, d, sems_out.at[i]) for i, (_, m, d) in enumerate(parts)]
+    for copy in ins:
         copy.start()
-    for copy in copies:
+    for first, second in zip(ins, outs):
+        first.wait()
+        second.start()
+    for copy in outs:
         copy.wait()
 
 
@@ -401,7 +428,7 @@
     rows_out = down_proj.shape[1]
     hi, ho = rows_in // 2, rows_out // 2
     total = nz * 2 * tok
-    copies = 16 * (nx + ny - 2) + nz
+    copies = 16 * (nx + ny - 2)
     V = pltpu.VMEM
     dma = pltpu.SemaphoreType.DMA
     e = EXP_DEV
@@ -435,7 +462,7 @@
             V((e, ny - 1, ho, width), BF16),
             V((nz, 2, tok, width + LANES), BF16),
             V((nz, tok, width + LANES), BF16),
-            V((nz - 1, tok, width + LANES), BF16),
+            V((nz, tok, width + LANES), BF16),
             dma((copies,)),
             dma((copies,)),
             dma((nz,)),
@@ -444,6 +471,10 @@
             dma((nz,)),
             dma((nz,)),
             dma((4,)),
+            dma((nz,)),
+            dma((nz,)),
+            dma((nz,)),
+            dma((nz,)),
         ],
         compiler_params=pltpu.CompilerParams(
             collective_id=0, has_side_effects=True, vmem_limit_bytes=60 * 2**20
@@ -458,7 +489,7 @@
         out_shape=tuple(jax.ShapeDtypeStruct(a.shape, a.dtype) for a in (gtok, ggu, gd)),
         in_specs=[pl.BlockSpec(memory_space=pl.ANY)] * 3,
         out_specs=[pl.BlockSpec(memory_space=pl.ANY)] * 3,
-        scratch_shapes=[dma((4 * e + 1,))],
+        scratch_shapes=[V(a.shape, a.dtype) for a in (gtok, ggu, gd)] + [dma((4 * e + 1,))] * 2,
         compiler_params=pltpu.CompilerParams(vmem_limit_bytes=60 * 2**20),
     )(gtok, ggu, gd)
     return gtok, ggate.astype(BF16).T, ggu, gd

time: 219 us -> 118 us (0.54)
  Pallas kernels: 218 us -> 116 us
    pallas_call x1, Pallas kernels: 104 us -> 2.93 us  [body(): pl.pallas_call(emit, out_shape=tuple((jax.ShapeDtypeStruct(a.shape, a.dty...]
where the time goes in v4:
time: 118 us; the launch traced here: 117 us
  Pallas kernels  116 us (98%)
    pallas_call x1, Pallas kernels, body(): pl.pallas_call(functools.partial(kernel, ny, nx, nz), out_shape=(jax.Shap...  113 us
    pallas_call x1, Pallas kernels, body(): pl.pallas_call(emit, out_shape=tuple((jax.ShapeDtypeStruct(a.shape, a.dty...  2.93 us

profile of v4, /device:TPU:0, one launch (start us, length us, event | category | flops | bytes accessed | tf_op | source)
XLA Modules:
  0.0 117.4 jit_solution(11046231549158195872)
XLA Ops:
  0.6 113.2 %shard_map.93 = (bf16[128,1024]{1,0:T(8,128)(2,1)}, f32[8,128]{1,0:T(8,128)}, f32[2,256,1024]{2,1,0:T(8,128)}, f32[2,128,1024]{2,1,0:T(8,128)}) custom-call(bf16[128,1024]{1,0:T(8,128)(2,1)} %x_ref.1, bf16[128,1024]{1,0:T(8,128)(2,1)} %dy_ref.1, s32[8,128]{1,0:T(8,128)} %bitcast.8, bf16[8,128]{1,0:T(8,128)(2,1)} %bitcast.9, ...), custom_call_target="tpu_custom_call" | custom-call | flops 17179869184 | bytes 8388608 | tf_op jit(solution)/shard_map/pallas_call | solution.py:436
  113.9 0.0 copy-start
  113.9 2.9 %shard_map.94 = (bf16[128,1024]{1,0:T(8,128)(2,1)}, f32[2,256,1024]{2,1,0:T(8,128)}, f32[2,128,1024]{2,1,0:T(8,128)}) custom-call(bf16[128,1024]{1,0:T(8,128)(2,1)} %get-tuple-element.11.gtok, f32[2,256,1024]{2,1,0:T(8,128)} %get-tuple-element.12.ggu, f32[2,128,1024]{2,1,0:T(8,128)} %get-tuple-element.13.gd), custom_call_target="tpu_custom_call" | custom-call | tf_op jit(solution)/shard_map/pallas_call | solution.py:487
  116.8 0.0 copy-done
  116.8 0.6 convert_bitcast_fusion
Async XLA Ops:
  113.9 3.0 %copy-start = (f32[8,128]{1,0:T(8,128)S(1)}, f32[8,128]{1,0:T(8,128)}, u32[]{:S(2)}) copy-start(f32[8,128]{1,0:T(8,128)} %get-tuple-element.15) | copy-start | bytes 12292

commit v5 on v4

--- a/solution.py
+++ b/solution.py
@@ -311,9 +311,10 @@
         chain_step(s)
     arrived(second0)
     first1 = weights_first(1)
-    lax.fori_loop(0, nz - 1, forward_arrived, 0)
+    lax.fori_loop(0, nz - 2, forward_arrived, 0)
     arrived(first1)
     second1 = weights_second(1)
+    forward_arrived(nz - 2, 0)
     chain_step(nz - 1)
     forward_arrived(nz - 1, 0)
     gradients_in(0)
@@ -324,9 +325,6 @@
     lax.fori_loop(0, nz // group, forward_all, 0)
     gradients_in(1)
     firsts1 = [sums_first(1, kinds[0])]
-    gradients_out(1)
-    firsts1.append(sums_first(1, kinds[1]))
-
     def dx_pair(to):
         return pltpu.make_async_remote_copy(
             src_ref=dxp.at[to, 1 - c], dst_ref=dx_r1.at[to],
@@ -359,7 +357,10 @@
         return carry
 
     lax.fori_loop(0, nz, dx_step, 0)
-    seconds0 = [sums_second(0, kind, first) for kind, first in zip(kinds, firsts0)]
+    seconds0 = [sums_second(0, kinds[0], firsts0[0])]
+    gradients_out(1)
+    firsts1.append(sums_first(1, kinds[1]))
+    seconds0.append(sums_second(0, kinds[1], firsts0[1]))
     seconds1 = [sums_second(1, kind, first) for kind, first in zip(kinds, firsts1)]
     for kind, second in zip(kinds, seconds0):
         sums_last(0, kind, second)

time: 118 us -> 118 us (level)
  no operation moved by 1% of the time
where the time goes in v5:
time: 118 us; the launch traced here: 117 us
  Pallas kernels  116 us (98%)
    pallas_call x1, Pallas kernels, body(): pl.pallas_call(functools.partial(kernel, ny, nx, nz), out_shape=(jax.Shap...  113 us
    pallas_call x1, Pallas kernels, body(): pl.pallas_call(emit, out_shape=tuple((jax.ShapeDtypeStruct(a.shape, a.dty...  2.93 us

profile of v5, /device:TPU:0, one launch (start us, length us, event | category | flops | bytes accessed | tf_op | source)
XLA Modules:
  0.0 117.4 jit_solution(6715657296404118942)
XLA Ops:
  0.6 113.2 %shard_map.93 = (bf16[128,1024]{1,0:T(8,128)(2,1)}, f32[8,128]{1,0:T(8,128)}, f32[2,256,1024]{2,1,0:T(8,128)}, f32[2,128,1024]{2,1,0:T(8,128)}) custom-call(bf16[128,1024]{1,0:T(8,128)(2,1)} %x_ref.1, bf16[128,1024]{1,0:T(8,128)(2,1)} %dy_ref.1, s32[8,128]{1,0:T(8,128)} %bitcast.8, bf16[8,128]{1,0:T(8,128)(2,1)} %bitcast.9, ...), custom_call_target="tpu_custom_call" | custom-call | flops 17179869184 | bytes 8388608 | tf_op jit(solution)/shard_map/pallas_call | solution.py:437
  113.9 0.0 copy-start
  113.9 2.9 %shard_map.94 = (bf16[128,1024]{1,0:T(8,128)(2,1)}, f32[2,256,1024]{2,1,0:T(8,128)}, f32[2,128,1024]{2,1,0:T(8,128)}) custom-call(bf16[128,1024]{1,0:T(8,128)(2,1)} %get-tuple-element.11.gtok, f32[2,256,1024]{2,1,0:T(8,128)} %get-tuple-element.12.ggu, f32[2,128,1024]{2,1,0:T(8,128)} %get-tuple-element.13.gd), custom_call_target="tpu_custom_call" | custom-call | tf_op jit(solution)/shard_map/pallas_call | solution.py:488
  116.8 0.0 copy-done
  116.8 0.6 convert_bitcast_fusion
Async XLA Ops:
  113.9 3.0 %copy-start = (f32[8,128]{1,0:T(8,128)S(1)}, f32[8,128]{1,0:T(8,128)}, u32[]{:S(2)}) copy-start(f32[8,128]{1,0:T(8,128)} %get-tuple-element.15) | copy-start | bytes 12292

commit v6 on v5

--- a/solution.py
+++ b/solution.py
@@ -178,6 +178,7 @@
     transpose(z, c)
     arrived(first0)
     second0 = weights_second(0)
+    first1 = weights_first(1)
 
     def forward(j, first, group):
         rows = group * 2 * tok
@@ -310,17 +311,16 @@
     for s in range(1, nz - 1):
         chain_step(s)
     arrived(second0)
-    first1 = weights_first(1)
     lax.fori_loop(0, nz - 2, forward_arrived, 0)
     arrived(first1)
     second1 = weights_second(1)
     forward_arrived(nz - 2, 0)
     chain_step(nz - 1)
     forward_arrived(nz - 1, 0)
+    gradients_out(0)
+    first_out = sums_first(0, kinds[1])
     gradients_in(0)
-    firsts0 = [sums_first(0, kinds[0])]
-    gradients_out(0)
-    firsts0.append(sums_first(0, kinds[1]))
+    firsts0 = [sums_first(0, kinds[0]), first_out]
     arrived(second1)
     lax.fori_loop(0, nz // group, forward_all, 0)
     gradients_in(1)

time: 118 us -> 118 us (level)
  no operation moved by 1% of the time
where the time goes in v6:
time: 118 us; the launch traced here: 117 us
  Pallas kernels  116 us (98%)
    pallas_call x1, Pallas kernels, body(): pl.pallas_call(functools.partial(kernel, ny, nx, nz), out_shape=(jax.Shap...  113 us
    pallas_call x1, Pallas kernels, body(): pl.pallas_call(emit, out_shape=tuple((jax.ShapeDtypeStruct(a.shape, a.dty...  2.93 us

profile of v6, /device:TPU:0, one launch (start us, length us, event | category | flops | bytes accessed | tf_op | source)
XLA Modules:
  0.0 117.4 jit_solution(5542620431386826132)
XLA Ops:
  0.6 113.2 %shard_map.93 = (bf16[128,1024]{1,0:T(8,128)(2,1)}, f32[8,128]{1,0:T(8,128)}, f32[2,256,1024]{2,1,0:T(8,128)}, f32[2,128,1024]{2,1,0:T(8,128)}) custom-call(bf16[128,1024]{1,0:T(8,128)(2,1)} %x_ref.1, bf16[128,1024]{1,0:T(8,128)(2,1)} %dy_ref.1, s32[8,128]{1,0:T(8,128)} %bitcast.8, bf16[8,128]{1,0:T(8,128)(2,1)} %bitcast.9, ...), custom_call_target="tpu_custom_call" | custom-call | flops 17179869184 | bytes 8388608 | tf_op jit(solution)/shard_map/pallas_call | solution.py:437
  113.9 0.0 copy-start
  113.9 2.9 %shard_map.94 = (bf16[128,1024]{1,0:T(8,128)(2,1)}, f32[2,256,1024]{2,1,0:T(8,128)}, f32[2,128,1024]{2,1,0:T(8,128)}) custom-call(bf16[128,1024]{1,0:T(8,128)(2,1)} %get-tuple-element.11.gtok, f32[2,256,1024]{2,1,0:T(8,128)} %get-tuple-element.12.ggu, f32[2,128,1024]{2,1,0:T(8,128)} %get-tuple-element.13.gd), custom_call_target="tpu_custom_call" | custom-call | tf_op jit(solution)/shard_map/pallas_call | solution.py:488
  116.8 0.0 copy-done
  116.8 0.6 convert_bitcast_fusion
Async XLA Ops:
  113.9 3.0 %copy-start = (f32[8,128]{1,0:T(8,128)S(1)}, f32[8,128]{1,0:T(8,128)}, u32[]{:S(2)}) copy-start(f32[8,128]{1,0:T(8,128)} %get-tuple-element.15) | copy-start | bytes 12292
